TPU v7x, 1024 devices: a whole 4x4x32 slice. The times are simulated.
1024 devices in a mesh: gx: 16 (over x, y_lo, core), gy: 64 (over z, y_hi).
Axes of the slice: x: 4, y: 4 (y_hi: 2, y_lo: 2; y = y_hi * 2 + y_lo), z: 32, core: 2. Of those that a mesh axis runs over, the one named last changes fastest.
Arguments:
- substrate: float32 [16, 512, 4096], P(None, 'gy', 'gx'), may hold values from 0 to 1
- catalyst: float32 [16, 512, 4096], P(None, 'gy', 'gx'), may hold values from 0 to 1
Outputs:
- substrate_next: float32 [16, 512, 4096], P(None, 'gy', 'gx')
- catalyst_next: float32 [16, 512, 4096], P(None, 'gy', 'gx')
- rebuilt: float32 [2, 16, 4096, 512], P(None, None, ('gx', 'gy'))
All inputs are finite; a program needn't handle non-finite values.
Results may differ from a plain program's by a relative error of at most 0.00002.
Values sent between devices are 32-bit elements; how exact they have to be, the bound alone decides.
No kernel may reach another device: no remote copies, remote signals or barrier semaphores. Data moves between devices by JAX's collectives and lax.ppermute only.
A program may use at most 32 MiB of HBM per device.

v0:
```python
import jax
import jax.numpy as jnp
from jax import lax
from jax.sharding import PartitionSpec as P

feed_rate = 0.037
kill_rate = 0.06
substrate_diffusion = 0.15
catalyst_diffusion = 0.08


def with_halo(shard, sides, width):
    for axis, dim in sides:
        size, length = (lax.axis_size(axis), shard.shape[dim])
        up = [(i, (i + 1) % size) for i in range(size)]
        down = [(j, i) for i, j in up]
        last = lax.slice_in_dim(shard, length - width, length, axis=dim)
        first = lax.slice_in_dim(shard, 0, width, axis=dim)
        before = lax.ppermute(last, axis, up)
        after = lax.ppermute(first, axis, down)
        shard = jnp.concatenate([before, shard, after], axis=dim)
    return shard


def side_by_side(arrays, axis, split_dim, concat_dim, along):
    both = jnp.concatenate(arrays, axis=along)
    result, at, outs = (
        lax.all_to_all(both, axis, split_axis=split_dim, concat_axis=concat_dim, tiled=True),
        0,
        [],
    )
    for a in arrays:
        outs.append(lax.slice_in_dim(result, at, at + a.shape[along], axis=along))
        at += a.shape[along]
    return tuple(outs)


def react(center, spread):
    substrate = center[0]
    catalyst = center[1]
    reaction = substrate * catalyst * catalyst
    new_substrate = (
        substrate + substrate_diffusion * spread[0] - reaction + feed_rate * (1.0 - substrate)
    )
    new_catalyst = (
        catalyst + catalyst_diffusion * spread[1] + reaction - (feed_rate + kill_rate) * catalyst
    )
    return jnp.stack([new_substrate, new_catalyst])


def advance(padded):
    center = padded[:, :, 1:-1, 1:-1]
    spread = jnp.roll(center, 1, 1) + jnp.roll(center, -1, 1)
    spread = spread + padded[:, :, 2:, 1:-1] + padded[:, :, :-2, 1:-1]
    spread = spread + padded[:, :, 1:-1, 2:] + padded[:, :, 1:-1, :-2]
    return react(center, spread - 6.0 * center)


def restrict(field):
    shape = field.shape
    blocks = field.reshape(shape[0], shape[1], shape[2] // 2, 2, shape[3] // 2, 2)
    return (
        blocks[:, :, :, 0, :, 0]
        + blocks[:, :, :, 0, :, 1]
        + blocks[:, :, :, 1, :, 0]
        + blocks[:, :, :, 1, :, 1]
    ) * 0.25


def prolong(field):
    return jnp.repeat(jnp.repeat(field, 2, axis=2), 2, axis=3)


def pack(level, owners):
    fields, planes, extent, columns = level.shape
    portion = columns // owners
    blocks = level.reshape(fields, planes, extent, owners, portion)
    blocks = jnp.transpose(blocks, (0, 3, 1, 4, 2))
    return blocks.reshape(fields, owners, planes * portion * extent)


def unpack(received, shape, owners):
    fields, planes, extent, columns = shape
    portion = columns // owners
    blocks = received.reshape(fields, owners, planes, portion, extent)
    blocks = jnp.transpose(blocks, (0, 2, 3, 1, 4))
    return blocks.reshape(fields, planes, portion, owners * extent)


def body(substrate, catalyst):
    state = jnp.stack([substrate, catalyst])
    padded = with_halo(state, (("gx", 3), ("gy", 2)), 2)
    state = advance(advance(padded))
    level1 = restrict(state)
    level2 = restrict(level1)
    owners = lax.axis_size("gy")
    detail = level1 - prolong(level2)
    got_detail, got_coarse = side_by_side(
        (pack(detail, owners), pack(level2, owners)), "gy", 1, 1, 2
    )
    coarse = prolong(unpack(got_coarse, level2.shape, owners))
    blend = coarse + 0.5 * unpack(got_detail, level1.shape, owners)
    rebuilt = prolong(blend)
    return (state[0], state[1], rebuilt)


def solution(mesh):
    in_specs = (P(None, "gy", "gx"), P(None, "gy", "gx"))
    out_specs = (P(None, "gy", "gx"), P(None, "gy", "gx"), P(None, None, ("gx", "gy"), None))
    return jax.shard_map(body, mesh=mesh, in_specs=in_specs, out_specs=out_specs, check_vma=False)
```

profile of v0, /device:TPU:4, one launch (start us, length us, event | category | flops | bytes accessed | tf_op | source)
XLA Modules:
  0.0 101.4 jit_solution(3906028888091178855)
XLA Ops:
  0.6 1.0 %fusion.26 = (f32[2,16,8,2]{3,2,1,0:T(8,128)S(1)}, f32[2,16,8,2]{3,2,1,0:T(8,128)S(1)}) fusion(f32[1,16,8,256]{3,2,1,0:T(8,128)} %bitcast.67, f32[1,16,8,256]{3,2,1,0:T(8,128)} %bitcast.71), kind=kLoop, calls=%fused_computation.80 | loop fusion | flops 1024 | bytes 266240 | tf_op jit(solution)/shard_map/stack | solution.py:91
  1.7 1.9 %collective-permute-start = (f32[2,16,8,2]{3,2,1,0:T(8,128)S(1)}, f32[2,16,8,2]{3,2,1,0:T(8,128)S(1)}, u32[]{:S(2)}, u32[]{:S(2)}) collective-permute-start(f32[2,16,8,2]{3,2,1,0:T(8,128)S(1)} %get-tuple-element.28), channel_id=1, source_target_pairs={{0,64},{64,128},{128,192},{192,256},{256,320},{320,384},{384,448},... | collective-permute-start | bytes 6152 | tf_op jit(solution)/shard_map/ppermute | solution.py:19
  3.6 4.5 %collective-permute-start.1 = (f32[2,16,8,2]{3,2,1,0:T(8,128)S(1)}, f32[2,16,8,2]{3,2,1,0:T(8,128)S(1)}, u32[]{:S(2)}, u32[]{:S(2)}) collective-permute-start(f32[2,16,8,2]{3,2,1,0:T(8,128)S(1)} %get-tuple-element.29), channel_id=1, source_target_pairs={{64,0},{128,64},{192,128},{256,192},{320,256},{384,320},{448,384},... | collective-permute-start | bytes 6152 | tf_op jit(solution)/shard_map/ppermute | solution.py:20
  8.1 0.7 collective-permute-done
  8.9 1.8 %collective-permute-done.1 = f32[2,16,8,2]{3,2,1,0:T(8,128)S(1)} collective-permute-done((f32[2,16,8,2]{3,2,1,0:T(8,128)S(1)}, f32[2,16,8,2]{3,2,1,0:T(8,128)S(1)}, u32[]{:S(2)}, u32[]{:S(2)}) %collective-permute-start.1) | collective-permute-done | bytes 2080 | tf_op jit(solution)/shard_map/ppermute | solution.py:20
  10.6 1.4 %pad_maximum_fusion.26 = (f32[2,16,2,260]{3,2,1,0:T(2,128)S(1)}, f32[2,16,2,260]{3,2,1,0:T(2,128)S(1)}) fusion(f32[2,16,8,2]{3,2,1,0:T(8,128)S(1)} %collective-permute-done.1, f32[2,16,8,2]{3,2,1,0:T(8,128)S(1)} %collective-permute-done, f32[1,16,8,256]{3,2,1,0:T(8,128)} %bitcast.72, f32[1,16,8,256]{3,2,1,0:T(8,128)} %bitcast.68), kind=kLoop, calls=%fused_computation.98 | loop fusion | flops 99840 | bytes 399360 | tf_op jit(solution)/shard_map/slice | solution.py:17
  12.1 5.1 %collective-permute-start.2 = (f32[2,16,2,260]{3,2,1,0:T(2,128)S(1)}, f32[2,16,2,260]{3,2,1,0:T(2,128)S(1)}, u32[]{:S(2)}, u32[]{:S(2)}) collective-permute-start(f32[2,16,2,260]{3,2,1,0:T(2,128)S(1)} %get-tuple-element.26), channel_id=1, source_target_pairs={{0,1},{1,2},{2,3},{3,4},{4,5},{5,6},{6,7},{7,8},{8,9},{9,10},{10,1... | collective-permute-start | bytes 199688 | tf_op jit(solution)/shard_map/ppermute | solution.py:19
  17.2 0.0 copy-start
  17.2 0.0 copy-start.1
  17.2 18.3 %collective-permute-start.3 = (f32[2,16,2,260]{3,2,1,0:T(2,128)S(1)}, f32[2,16,2,260]{3,2,1,0:T(2,128)S(1)}, u32[]{:S(2)}, u32[]{:S(2)}) collective-permute-start(f32[2,16,2,260]{3,2,1,0:T(2,128)S(1)} %get-tuple-element.27), channel_id=1, source_target_pairs={{1,0},{2,1},{3,2},{4,3},{5,4},{6,5},{7,6},{8,7},{9,8},{10,9},{11,1... | collective-permute-start | bytes 199688 | tf_op jit(solution)/shard_map/ppermute | solution.py:20
  35.5 1.5 %collective-permute-done.2 = f32[2,16,2,260]{3,2,1,0:T(2,128)S(1)} collective-permute-done((f32[2,16,2,260]{3,2,1,0:T(2,128)S(1)}, f32[2,16,2,260]{3,2,1,0:T(2,128)S(1)}, u32[]{:S(2)}, u32[]{:S(2)}) %collective-permute-start.2) | collective-permute-done | bytes 66592 | tf_op jit(solution)/shard_map/ppermute | solution.py:19
  37.0 1.3 %collective-permute-done.3 = f32[2,16,2,260]{3,2,1,0:T(2,128)S(1)} collective-permute-done((f32[2,16,2,260]{3,2,1,0:T(2,128)S(1)}, f32[2,16,2,260]{3,2,1,0:T(2,128)S(1)}, u32[]{:S(2)}, u32[]{:S(2)}) %collective-permute-start.3) | collective-permute-done | bytes 66592 | tf_op jit(solution)/shard_map/ppermute | solution.py:20
  38.3 1.3 %pad_maximum_fusion.18 = f32[2,16,12,260]{3,2,1,0:T(8,128)S(1)} fusion(f32[2,16,2,260]{3,2,1,0:T(2,128)S(1)} %collective-permute-done.3, f32[2,16,8,2]{3,2,1,0:T(8,128)S(1)} %collective-permute-done.1, f32[1,16,8,256]{3,2,1,0:T(8,128)} %bitcast.73, f32[1,16,8,256]{3,2,1,0:T(8,128)} %bitcast.69, f32[2,16,8,2]{3,2,1,0:T(8,128)S(1)} %collective-permute-done, ...), kind=kLoop, calls=%fused_computation.41 | loop fusion | flops 499200 | bytes 798720 | tf_op jit(solution)/shard_map/concatenate | solution.py:21
  39.6 0.5 fusion.40
  40.1 0.0 copy-done
  40.1 0.0 copy-done.1
  40.1 1.3 %fusion = f32[2,16,10,258]{3,2,1,0:T(8,128)S(1)} fusion(f32[2,16,12,260]{3,2,1,0:T(8,128)S(1)} %pad_maximum_fusion.18, f32[2,16,2,260]{3,2,1,0:T(2,128)S(1)} %collective-permute-done.2, f32[2,16,8,2]{3,2,1,0:T(8,128)S(1)} %collective-permute-done.1, f32[2,16,8,2]{3,2,1,0:T(8,128)S(1)} %collective-permute-done, f32[1,16,8,256]{3,2,1,0:T(8,128)S(1)} %bitcast.74, ...), kind=kLoop, calls=%fused_computation.15 | loop fusion | flops 2229120 | bytes 2339520 | tf_op jit(solution)/shard_map/sub | solution.py:56
  41.4 0.3 fusion.8
  41.7 0.1 fusion.39
  41.8 0.2 fusion.25
  42.0 0.4 fusion.14
  42.4 0.1 multiply_subtract_fusion
  42.5 0.3 copy.34
  42.9 0.4 copy.36
  43.3 0.4 copy.33
  43.6 0.4 copy.35
  44.1 0.2 copy.37
  44.3 0.5 fusion.41
  44.8 0.1 copy.53
  44.9 0.1 copy.54
  45.0 0.1 copy.52
  45.1 0.1 copy.55
  45.2 0.1 copy.43
  45.3 0.3 subtract_bitcast_fusion
  45.6 0.2 copy.44
  45.9 0.8 copy.46
  46.6 19.0 %all-to-all-start = ((f32[2,64,160]{2,0,1:T(2,128)}), f32[2,64,160]{2,0,1:T(2,128)S(1)}, u32[]{:S(2)}, u32[]{:S(2)}) async-start(f32[2,64,160]{2,0,1:T(2,128)} %copy.46), calls=%async_computation | async-start | bytes 262144 | tf_op jit(solution)/shard_map/all_to_all | solution.py:28
  65.7 0.8 fusion.28
  66.5 32.0 %all-to-all-done = f32[2,64,160]{2,0,1:T(2,128)S(1)} async-done(((f32[2,64,160]{2,0,1:T(2,128)}), f32[2,64,160]{2,0,1:T(2,128)S(1)}, u32[]{:S(2)}, u32[]{:S(2)}) %all-to-all-start) | async-done | bytes 81952 | tf_op jit(solution)/shard_map/all_to_all | solution.py:28
  98.6 0.1 copy.56
  98.7 0.1 copy.57
  98.8 0.1 copy.48
  98.9 0.2 copy.50
  99.2 0.1 broadcast_in_dim.22
  99.3 0.1 broadcast_add_fusion
  99.3 0.1 broadcast_in_dim.25
  99.4 0.7 broadcast_in_dim.26
  100.1 1.3 %copy.51 = f32[2,16,4,512]{3,2,1,0:T(4,128)} copy(f32[2,16,4,512]{1,3,2,0:T(8,128)S(1)} %bitcast.60) | data formatting | bytes 524288
  (8 shorter events, 0.2 us)
Async XLA Ops:
  1.7 7.2 %collective-permute-start = (f32[2,16,8,2]{3,2,1,0:T(8,128)S(1)}, f32[2,16,8,2]{3,2,1,0:T(8,128)S(1)}, u32[]{:S(2)}, u32[]{:S(2)}) collective-permute-start(f32[2,16,8,2]{3,2,1,0:T(8,128)S(1)} %get-tuple-element.28), channel_id=1, source_target_pairs={{0,64},{64,128},{128,192},{192,256},{256,320},{320,384},{384,448},... | collective-permute-start | bytes 6152 | tf_op jit(solution)/shard_map/ppermute | solution.py:19
  3.6 7.0 %collective-permute-start.1 = (f32[2,16,8,2]{3,2,1,0:T(8,128)S(1)}, f32[2,16,8,2]{3,2,1,0:T(8,128)S(1)}, u32[]{:S(2)}, u32[]{:S(2)}) collective-permute-start(f32[2,16,8,2]{3,2,1,0:T(8,128)S(1)} %get-tuple-element.29), channel_id=1, source_target_pairs={{64,0},{128,64},{192,128},{256,192},{320,256},{384,320},{448,384},... | collective-permute-start | bytes 6152 | tf_op jit(solution)/shard_map/ppermute | solution.py:20
  12.1 24.9 %collective-permute-start.2 = (f32[2,16,2,260]{3,2,1,0:T(2,128)S(1)}, f32[2,16,2,260]{3,2,1,0:T(2,128)S(1)}, u32[]{:S(2)}, u32[]{:S(2)}) collective-permute-start(f32[2,16,2,260]{3,2,1,0:T(2,128)S(1)} %get-tuple-element.26), channel_id=1, source_target_pairs={{0,1},{1,2},{2,3},{3,4},{4,5},{5,6},{6,7},{7,8},{8,9},{9,10},{10,1... | collective-permute-start | bytes 199688 | tf_op jit(solution)/shard_map/ppermute | solution.py:19
  17.2 22.9 %copy-start = (f32[16,8,256]{2,1,0:T(8,128)S(1)}, f32[16,8,256]{2,1,0:T(8,128)}, u32[]{:S(2)}) copy-start(f32[16,8,256]{2,1,0:T(8,128)} %param.2) | copy-start | bytes 393220
  17.2 22.9 %copy-start.1 = (f32[16,8,256]{2,1,0:T(8,128)S(1)}, f32[16,8,256]{2,1,0:T(8,128)}, u32[]{:S(2)}) copy-start(f32[16,8,256]{2,1,0:T(8,128)} %param.3) | copy-start | bytes 393220
  17.2 21.1 %collective-permute-start.3 = (f32[2,16,2,260]{3,2,1,0:T(2,128)S(1)}, f32[2,16,2,260]{3,2,1,0:T(2,128)S(1)}, u32[]{:S(2)}, u32[]{:S(2)}) collective-permute-start(f32[2,16,2,260]{3,2,1,0:T(2,128)S(1)} %get-tuple-element.27), channel_id=1, source_target_pairs={{1,0},{2,1},{3,2},{4,3},{5,4},{6,5},{7,6},{8,7},{9,8},{10,9},{11,1... | collective-permute-start | bytes 199688 | tf_op jit(solution)/shard_map/ppermute | solution.py:20
  46.6 51.9 %all-to-all-start = ((f32[2,64,160]{2,0,1:T(2,128)}), f32[2,64,160]{2,0,1:T(2,128)S(1)}, u32[]{:S(2)}, u32[]{:S(2)}) async-start(f32[2,64,160]{2,0,1:T(2,128)} %copy.46), calls=%async_computation | async-start | bytes 262144 | tf_op jit(solution)/shard_map/all_to_all | solution.py:28
where the time goes:
time: 102 us; the launch traced here: 101 us
  starting transfers between devices  48.8 us (48%)
  waiting for transfers between devices  37.4 us (37%)
  other arithmetic  7.43 us (7%)
  local copies, waits for them, and re-layouts  6.9 us (7%)
    all_to_all x1, waiting for transfers between devices, side_by_side(): lax.all_to_all(both, axis, split_axis=split_dim, concat_axis=concat_dim,...  32 us
    ppermute x2, starting transfers between devices, with_halo(): after = lax.ppermute(first, axis, down)  22.8 us
    all_to_all x1, starting transfers between devices, side_by_side(): lax.all_to_all(both, axis, split_axis=split_dim, concat_axis=concat_dim,...  19 us
    ppermute x2, starting transfers between devices, with_halo(): before = lax.ppermute(last, axis, up)  7.02 us
    ppermute x2, waiting for transfers between devices, with_halo(): after = lax.ppermute(first, axis, down)  3.13 us
    ppermute x2, waiting for transfers between devices, with_halo(): before = lax.ppermute(last, axis, up)  2.19 us
  transfers between devices with their start and end apart: 5, of which 5 were waited for; matrix products, arithmetic and copies ran while one was open for 1% of the time, Pallas kernels for 0%

commit v1 on v0

v1 whole, which is shorter than its diff:
```python
import jax
import jax.numpy as jnp
from jax import lax
from jax.experimental import pallas as pl
from jax.experimental.pallas import tpu as pltpu
from jax.sharding import PartitionSpec as P

feed_rate = 0.037
kill_rate = 0.06
substrate_diffusion = 0.15
catalyst_diffusion = 0.08

planes, cols, rows = 16, 8, 256
owners = 64
f32 = jnp.float32


def lane_ids(shape):
    return lax.broadcasted_iota(jnp.int32, shape, len(shape) - 1)


def slice_kernel(u_ref, v_ref, first_ref, last_ref):
    for f, ref in enumerate((u_ref, v_ref)):
        first_ref[f] = ref[:, 0:2, :]
        last_ref[f] = ref[:, cols - 2 : cols, :]


def edge_kernel(u_ref, v_ref, before_ref, after_ref, edge_ref, pad_ref):
    lane = lane_ids((16, 128))
    low = lane < 64
    here = (lane < 2) | (lane >= 126)
    packed = jnp.zeros((16, 128), f32)
    for f, ref in enumerate((u_ref, v_ref)):
        for p in range(planes):
            q = f * planes + p
            for t, lanes in enumerate((slice(0, 128), slice(rows - 128, rows))):
                pad_ref[q, t, 0:8, :] = ref[p, :, lanes]
                pad_ref[q, t, 8:10, :] = after_ref[f, p, :, lanes]
                pad_ref[q, t, 14:16, :] = before_ref[f, p, :, lanes]
    for q in range(2 * planes):
        both = jnp.where(low, pad_ref[q, 0], pad_ref[q, 1])
        moved = pltpu.roll(jnp.where(here, both, 0.0), 4 * q % 128, 1)
        packed = packed + moved
    row = lax.broadcasted_iota(jnp.int32, (16, 128), 0)
    edge_ref[...] = jnp.where((row < 10) | (row >= 14), packed, 0.0)


def neighbours(x, below, above):
    n, m = x.shape
    total = below + above
    total = total + pltpu.roll(x, 1, 0) + pltpu.roll(x, n - 1, 0)
    total = total + pltpu.roll(x, 1, 1) + pltpu.roll(x, m - 1, 1)
    return total - 6.0 * x


def react(u, v, spread_u, spread_v):
    reaction = u * v * v
    new_u = u + substrate_diffusion * spread_u - reaction + feed_rate * (1.0 - u)
    new_v = v + catalyst_diffusion * spread_v + reaction - (feed_rate + kill_rate) * v
    return new_u, new_v


def step_kernel(
    u_ref, v_ref, before_ref, after_ref, left_ref, right_ref,
    un_ref, vn_ref, send_ref, pad_ref, mid_ref, done_ref, turn_ref,
):
    lane = lane_ids((16, 128))
    beside = jnp.where(lane % 4 < 2, right_ref[...], left_ref[...])
    for f, ref in enumerate((u_ref, v_ref)):
        pad_ref[f, :, 10:14, 0:rows] = jnp.zeros((planes, 4, rows), f32)
        pad_ref[f, :, 0:8, 0:rows] = ref[...]
        pad_ref[f, :, 8:10, 0:rows] = after_ref[f]
        pad_ref[f, :, 14:16, 0:rows] = before_ref[f]
        for p in range(planes):
            q = f * planes + p
            pad_ref[f, p, :, rows : rows + 128] = pltpu.roll(beside, (128 - 4 * q) % 128, 1)

    for p in range(planes):
        below, above = (p - 1) % planes, (p + 1) % planes
        u, v = pad_ref[0, p], pad_ref[1, p]
        spread_u = neighbours(u, pad_ref[0, below], pad_ref[0, above])
        spread_v = neighbours(v, pad_ref[1, below], pad_ref[1, above])
        new_u, new_v = react(u, v, spread_u, spread_v)
        mid_ref[0, p] = new_u
        mid_ref[1, p] = new_v

    for p in range(planes):
        below, above = (p - 1) % planes, (p + 1) % planes
        u, v = mid_ref[0, p], mid_ref[1, p]
        spread_u = neighbours(u, mid_ref[0, below], mid_ref[0, above])
        spread_v = neighbours(v, mid_ref[1, below], mid_ref[1, above])
        new_u, new_v = react(u, v, spread_u, spread_v)
        for f, (ref, new) in enumerate(((un_ref, new_u), (vn_ref, new_v))):
            ref[p] = new[0:8, 0:rows]
            at = 8 * (f * planes + p)
            for t in range(2):
                done_ref[t, at : at + 8, :] = new[0:8, 128 * t : 128 * t + 128]

    many = 2 * planes
    for t in range(2):
        pairs = []
        for c in range(cols // 2):
            one = done_ref[t, pl.ds(2 * c, many, stride=8), :]
            two = done_ref[t, pl.ds(2 * c + 1, many, stride=8), :]
            pairs.append(one + two)
        turn_ref[128 * t : 128 * t + 128, :] = jnp.concatenate(pairs, axis=0).T
    lane = lane_ids((owners, 128))
    r0 = 0.25 * (turn_ref[pl.ds(0, owners, stride=4), :] + turn_ref[pl.ds(1, owners, stride=4), :])
    r1 = 0.25 * (turn_ref[pl.ds(2, owners, stride=4), :] + turn_ref[pl.ds(3, owners, stride=4), :])
    half = owners // 2
    for c1, out in enumerate((
        jnp.where(lane < 64, r0, pltpu.roll(r1, 64, 1)),
        jnp.where(lane < 64, pltpu.roll(r0, 64, 1), r1),
    )):
        send_ref[pl.ds(c1, half, stride=2), :] = out[half:]
        send_ref[pl.ds(2 * half + c1, half, stride=2), :] = out[:half]


def rebuild_kernel(got_ref, out_ref, wide_ref):
    level1 = got_ref[...]
    total = level1 + pltpu.roll(level1, 64, 1)
    coarse = 0.25 * (total + pltpu.roll(total, 32, 1))
    blend = coarse + 0.5 * (level1 - coarse)
    blend = jnp.concatenate([blend[64:], blend[:64]], axis=0)
    odd = pltpu.roll(blend, 96, 1)
    for d in range(2):
        wide_ref[pl.ds(d, 128, stride=4), :] = blend
        wide_ref[pl.ds(2 + d, 128, stride=4), :] = odd
    for t in range(4):
        turned = wide_ref[128 * t : 128 * t + 128, :].T
        for r in range(2):
            part = turned[64 * r : 64 * r + 32]
            for d in range(2):
                out_ref[pl.ds(4 * t + 2 * r + d, 32, stride=16), :] = part


def call(kernel, out_shape, scratch=()):
    return pl.pallas_call(
        kernel,
        out_shape=out_shape,
        scratch_shapes=[pltpu.VMEM(s, f32) for s in scratch],
        compiler_params=pltpu.CompilerParams(vmem_limit_bytes=32 * 1024 * 1024),
    )


def shape(*dims):
    return jax.ShapeDtypeStruct(dims, f32)


def ring(axis, by):
    size = lax.axis_size(axis)
    return [(i, (i + by) % size) for i in range(size)]


def body(u, v):
    column_halo = shape(2, planes, 2, rows)
    first, last = call(slice_kernel, (column_halo, column_halo))(u, v)
    before = lax.ppermute(last, "gy", ring("gy", 1))
    after = lax.ppermute(first, "gy", ring("gy", -1))
    edge = call(edge_kernel, shape(16, 128), [(2 * planes, 2, 16, 128)])(u, v, before, after)
    left = lax.ppermute(edge, "gx", ring("gx", 1))
    right = lax.ppermute(edge, "gx", ring("gx", -1))
    brick = shape(planes, cols, rows)
    padded = (2, planes, 16, rows + 128)
    un, vn, send = call(
        step_kernel, (brick, brick, shape(128, 128)), [padded, padded, (2, 256, 128), (rows, 128)]
    )(u, v, before, after, left, right)
    order = [(i + owners // 2) % owners for i in range(owners)]
    got = lax.all_to_all(
        send.reshape(owners, 2, 128), "gy", 0, 0, tiled=True, axis_index_groups=[order]
    )
    out = call(rebuild_kernel, shape(512, 128), [(512, 128)])(got.reshape(128, 128))
    out = out.reshape(2, planes, 4, 4, 128).transpose(0, 1, 3, 2, 4).reshape(2, planes, 4, 512)
    return un, vn, out


def solution(mesh):
    in_specs = (P(None, "gy", "gx"), P(None, "gy", "gx"))
    out_specs = (P(None, "gy", "gx"), P(None, "gy", "gx"), P(None, None, ("gx", "gy"), None))
    return jax.shard_map(body, mesh=mesh, in_specs=in_specs, out_specs=out_specs, check_vma=False)
```

time: 102 us -> 73.4 us (0.72)
  the two profiles are of different devices: /device:TPU:4 before, /device:TPU:32 now
where the time goes in v1:
time: 73.4 us; the launch traced here: 73.1 us
  blocking collectives  45.2 us (62%)
  starting transfers between devices  13 us (18%)
  waiting for transfers between devices  9.66 us (13%)
  Pallas kernels  2.81 us (4%)
  local copies, waits for them, and re-layouts  1.8 us (2%)
    all_to_all x1, blocking collectives, body(): lax.all_to_all(send.reshape(owners, 2, 128), 'gy', 0, 0, tiled=True, axis...  45.2 us
    ppermute x1, waiting for transfers between devices, body(): left = lax.ppermute(edge, 'gx', ring('gx', 1))  5.14 us
    ppermute x1, starting transfers between devices, body(): before = lax.ppermute(last, 'gy', ring('gy', 1))  5.1 us
    ppermute x1, waiting for transfers between devices, body(): after = lax.ppermute(first, 'gy', ring('gy', -1))  4.21 us
    ppermute x1, starting transfers between devices, body(): after = lax.ppermute(first, 'gy', ring('gy', -1))  3.14 us
    ppermute x1, starting transfers between devices, body(): right = lax.ppermute(edge, 'gx', ring('gx', -1))  2.79 us
    ppermute x1, starting transfers between devices, body(): left = lax.ppermute(edge, 'gx', ring('gx', 1))  1.92 us
    unnamed x4, local copies, waits for them, and re-layouts  1.8 us
  transfers between devices with their start and end apart: 4, of which 3 were waited for; matrix products, arithmetic and copies ran while one was open for 0% of the time, Pallas kernels for 0%

profile of v1, /device:TPU:32, one launch (start us, length us, event | category | flops | bytes accessed | tf_op | source)
XLA Modules:
  0.0 73.1 jit_solution(8705647565955384003)
XLA Ops:
  0.6 0.0 copy-start
  0.6 0.9 %copy-done = f32[16,8,256]{2,1,0:T(8,128)S(1)} copy-done((f32[16,8,256]{2,1,0:T(8,128)S(1)}, f32[16,8,256]{2,1,0:T(8,128)}, u32[]{:S(2)}) %copy-start) | copy-done | bytes 131096
  1.5 0.0 copy-start.1
  1.5 0.9 %copy-done.1 = f32[16,8,256]{2,1,0:T(8,128)S(1)} copy-done((f32[16,8,256]{2,1,0:T(8,128)S(1)}, f32[16,8,256]{2,1,0:T(8,128)}, u32[]{:S(2)}) %copy-start.1) | copy-done | bytes 131096
  2.5 5.1 %collective-permute-start = (f32[2,16,2,256]{3,2,1,0:T(2,128)S(1)}, f32[2,16,2,256]{3,2,1,0:T(2,128)S(1)}, u32[]{:S(2)}, u32[]{:S(2)}) collective-permute-start(f32[2,16,2,256]{3,2,1,0:T(2,128)S(1)} %get-tuple-element.8), channel_id=1, source_target_pairs={{0,1},{1,2},{2,3},{3,4},{4,5},{5,6},{6,7},{7,8},{8,9},{9,10},{10,1... | collective-permute-start | bytes 196616 | tf_op jit(solution)/shard_map/ppermute | solution.py:158
  7.6 3.1 %collective-permute-start.1 = (f32[2,16,2,256]{3,2,1,0:T(2,128)S(1)}, f32[2,16,2,256]{3,2,1,0:T(2,128)S(1)}, u32[]{:S(2)}, u32[]{:S(2)}) collective-permute-start(f32[2,16,2,256]{3,2,1,0:T(2,128)S(1)} %get-tuple-element.9), channel_id=1, source_target_pairs={{0,63},{1,0},{2,1},{3,2},{4,3},{5,4},{6,5},{7,6},{8,7},{9,8},{10,9... | collective-permute-start | bytes 196616 | tf_op jit(solution)/shard_map/ppermute | solution.py:159
  10.7 0.3 collective-permute-done.before_ref
  11.1 4.2 %collective-permute-done.1.after_ref = f32[2,16,2,256]{3,2,1,0:T(2,128)S(1)} collective-permute-done((f32[2,16,2,256]{3,2,1,0:T(2,128)S(1)}, f32[2,16,2,256]{3,2,1,0:T(2,128)S(1)}, u32[]{:S(2)}, u32[]{:S(2)}) %collective-permute-start.1) | collective-permute-done | bytes 65568 | tf_op jit(solution)/shard_map/ppermute | solution.py:159
  15.3 0.2 shard_map.50
  15.4 2.8 %collective-permute-start.3 = (f32[16,128]{1,0:T(8,128)S(1)}, f32[16,128]{1,0:T(8,128)S(1)}, u32[]{:S(2)}, u32[]{:S(2)}) collective-permute-start(f32[16,128]{1,0:T(8,128)S(1)} %shard_map.50), channel_id=1, source_target_pairs={{0,960},{64,0},{128,64},{192,128},{256,192},{320,256},{384,320},{4... | collective-permute-start | bytes 24584 | tf_op jit(solution)/shard_map/ppermute | solution.py:162
  18.2 1.9 %collective-permute-start.2 = (f32[16,128]{1,0:T(8,128)S(1)}, f32[16,128]{1,0:T(8,128)S(1)}, u32[]{:S(2)}, u32[]{:S(2)}) collective-permute-start(f32[16,128]{1,0:T(8,128)S(1)} %shard_map.50), channel_id=1, source_target_pairs={{0,64},{64,128},{128,192},{192,256},{256,320},{320,384},{384,448},... | collective-permute-start | bytes 24584 | tf_op jit(solution)/shard_map/ppermute | solution.py:161
  20.1 0.0 collective-permute-done.3.right_ref
  20.2 5.1 %collective-permute-done.2.left_ref = f32[16,128]{1,0:T(8,128)S(1)} collective-permute-done((f32[16,128]{1,0:T(8,128)S(1)}, f32[16,128]{1,0:T(8,128)S(1)}, u32[]{:S(2)}, u32[]{:S(2)}) %collective-permute-start.2) | collective-permute-done | bytes 8224 | tf_op jit(solution)/shard_map/ppermute | solution.py:161
  25.3 1.5 %shard_map.51 = (f32[16,8,256]{2,1,0:T(8,128)}, f32[16,8,256]{2,1,0:T(8,128)}, f32[128,128]{1,0:T(8,128)S(1)}) custom-call(f32[16,8,256]{2,1,0:T(8,128)S(1)} %copy-done, f32[16,8,256]{2,1,0:T(8,128)S(1)} %copy-done.1, f32[2,16,2,256]{3,2,1,0:T(2,128)S(1)} %collective-permute-done.before_ref, f32[2,16,2,256]{3,2,1,0:T(2,128)S(1)} %collective-permute-done.1.after_ref, ...), custom_call_target="tpu_custom_call" | custom-call | tf_op jit(solution)/shard_map/pallas_call | solution.py:165
  26.8 45.2 %all_to_all.5 = f32[64,2,128]{2,1,0:T(2,128)S(1)} all-to-all(f32[64,2,128]{2,1,0:T(2,128)S(1)} %bitcast.8), channel_id=1, replica_groups={{32,33,34,35,36,37,38,39,40,41,42,43,44,45,46,47,48,49,50,51,52,53,54,5..., dimensions={0} | all-to-all | bytes 131072 | tf_op jit(solution)/shard_map/all_to_all | solution.py:169
  72.0 1.1 %shard_map.52 = f32[512,128]{1,0:T(8,128)} custom-call(f32[128,128]{1,0:T(8,128)S(1)} %bitcast.7), custom_call_target="tpu_custom_call" | custom-call | tf_op jit(solution)/shard_map/pallas_call | solution.py:172
  (1 shorter events, 0.0 us)
Async XLA Ops:
  0.6 0.9 %copy-start = (f32[16,8,256]{2,1,0:T(8,128)S(1)}, f32[16,8,256]{2,1,0:T(8,128)}, u32[]{:S(2)}) copy-start(f32[16,8,256]{2,1,0:T(8,128)} %u_ref.5) | copy-start | bytes 393220
  1.5 0.9 %copy-start.1 = (f32[16,8,256]{2,1,0:T(8,128)S(1)}, f32[16,8,256]{2,1,0:T(8,128)}, u32[]{:S(2)}) copy-start(f32[16,8,256]{2,1,0:T(8,128)} %v_ref.5) | copy-start | bytes 393220
  2.5 8.6 %collective-permute-start = (f32[2,16,2,256]{3,2,1,0:T(2,128)S(1)}, f32[2,16,2,256]{3,2,1,0:T(2,128)S(1)}, u32[]{:S(2)}, u32[]{:S(2)}) collective-permute-start(f32[2,16,2,256]{3,2,1,0:T(2,128)S(1)} %get-tuple-element.8), channel_id=1, source_target_pairs={{0,1},{1,2},{2,3},{3,4},{4,5},{5,6},{6,7},{7,8},{8,9},{9,10},{10,1... | collective-permute-start | bytes 196616 | tf_op jit(solution)/shard_map/ppermute | solution.py:158
  7.6 7.7 %collective-permute-start.1 = (f32[2,16,2,256]{3,2,1,0:T(2,128)S(1)}, f32[2,16,2,256]{3,2,1,0:T(2,128)S(1)}, u32[]{:S(2)}, u32[]{:S(2)}) collective-permute-start(f32[2,16,2,256]{3,2,1,0:T(2,128)S(1)} %get-tuple-element.9), channel_id=1, source_target_pairs={{0,63},{1,0},{2,1},{3,2},{4,3},{5,4},{6,5},{7,6},{8,7},{9,8},{10,9... | collective-permute-start | bytes 196616 | tf_op jit(solution)/shard_map/ppermute | solution.py:159
  15.4 4.7 %collective-permute-start.3 = (f32[16,128]{1,0:T(8,128)S(1)}, f32[16,128]{1,0:T(8,128)S(1)}, u32[]{:S(2)}, u32[]{:S(2)}) collective-permute-start(f32[16,128]{1,0:T(8,128)S(1)} %shard_map.50), channel_id=1, source_target_pairs={{0,960},{64,0},{128,64},{192,128},{256,192},{320,256},{384,320},{4... | collective-permute-start | bytes 24584 | tf_op jit(solution)/shard_map/ppermute | solution.py:162
  18.2 7.1 %collective-permute-start.2 = (f32[16,128]{1,0:T(8,128)S(1)}, f32[16,128]{1,0:T(8,128)S(1)}, u32[]{:S(2)}, u32[]{:S(2)}) collective-permute-start(f32[16,128]{1,0:T(8,128)S(1)} %shard_map.50), channel_id=1, source_target_pairs={{0,64},{64,128},{128,192},{192,256},{256,320},{320,384},{384,448},... | collective-permute-start | bytes 24584 | tf_op jit(solution)/shard_map/ppermute | solution.py:161

commit v2 on v1

--- a/solution.py
+++ b/solution.py
@@ -12,6 +12,8 @@
 
 planes, cols, rows = 16, 8, 256
 owners = 64
+large = 56 * 1024 * 1024
+master = 37
 f32 = jnp.float32
 
 
@@ -19,24 +21,44 @@
     return lax.broadcasted_iota(jnp.int32, shape, len(shape) - 1)
 
 
-def slice_kernel(u_ref, v_ref, first_ref, last_ref):
-    for f, ref in enumerate((u_ref, v_ref)):
-        first_ref[f] = ref[:, 0:2, :]
-        last_ref[f] = ref[:, cols - 2 : cols, :]
-
-
-def edge_kernel(u_ref, v_ref, before_ref, after_ref, edge_ref, pad_ref):
+def odd(axis):
+    return lax.axis_index(axis) % 2 == 1
+
+
+def slice_kernel(u_hbm, v_hbm, one_ref, two_ref, u_ref, v_ref, sems):
+    part = planes // 2
+    copies = []
+    for f, (src, dst) in enumerate(((u_hbm, u_ref), (v_hbm, v_ref))):
+        for h in range(2):
+            at = pl.ds(h * part, part)
+            copies.append((f, h, pltpu.make_async_copy(src.at[at], dst.at[at], sems.at[f, h])))
+    for _, _, copy in copies:
+        copy.start()
+    second = odd("gy")
+    for f, h, copy in copies:
+        copy.wait()
+        at = slice(h * part, h * part + part)
+        ref = (u_ref, v_ref)[f]
+        first, last = ref[at, 0:2, :], ref[at, cols - 2 : cols, :]
+        one_ref[f, at] = jnp.where(second, first, last)
+        two_ref[f, at] = jnp.where(second, last, first)
+
+
+def edge_kernel(u_ref, v_ref, one_ref, two_ref, edge_ref, pad_ref):
     lane = lane_ids((16, 128))
     low = lane < 64
     here = (lane < 2) | (lane >= 126)
     packed = jnp.zeros((16, 128), f32)
+    second = odd("gy")
     for f, ref in enumerate((u_ref, v_ref)):
         for p in range(planes):
+            one, two = one_ref[f, p], two_ref[f, p]
+            after, before = jnp.where(second, two, one), jnp.where(second, one, two)
             q = f * planes + p
             for t, lanes in enumerate((slice(0, 128), slice(rows - 128, rows))):
                 pad_ref[q, t, 0:8, :] = ref[p, :, lanes]
-                pad_ref[q, t, 8:10, :] = after_ref[f, p, :, lanes]
-                pad_ref[q, t, 14:16, :] = before_ref[f, p, :, lanes]
+                pad_ref[q, t, 8:10, :] = after[:, lanes]
+                pad_ref[q, t, 14:16, :] = before[:, lanes]
     for q in range(2 * planes):
         both = jnp.where(low, pad_ref[q, 0], pad_ref[q, 1])
         moved = pltpu.roll(jnp.where(here, both, 0.0), 4 * q % 128, 1)
@@ -61,16 +83,18 @@
 
 
 def step_kernel(
-    u_ref, v_ref, before_ref, after_ref, left_ref, right_ref,
+    u_ref, v_ref, one_ref, two_ref, near_ref, far_ref,
     un_ref, vn_ref, send_ref, pad_ref, mid_ref, done_ref, turn_ref,
 ):
-    lane = lane_ids((16, 128))
-    beside = jnp.where(lane % 4 < 2, right_ref[...], left_ref[...])
+    right = lane_ids((16, 128)) % 4 < 2
+    beside = jnp.where(right != odd("gx"), near_ref[...], far_ref[...])
+    second = odd("gy")
     for f, ref in enumerate((u_ref, v_ref)):
         pad_ref[f, :, 10:14, 0:rows] = jnp.zeros((planes, 4, rows), f32)
         pad_ref[f, :, 0:8, 0:rows] = ref[...]
-        pad_ref[f, :, 8:10, 0:rows] = after_ref[f]
-        pad_ref[f, :, 14:16, 0:rows] = before_ref[f]
+        one, two = one_ref[f], two_ref[f]
+        pad_ref[f, :, 8:10, 0:rows] = jnp.where(second, two, one)
+        pad_ref[f, :, 14:16, 0:rows] = jnp.where(second, one, two)
         for p in range(planes):
             q = f * planes + p
             pad_ref[f, p, :, rows : rows + 128] = pltpu.roll(beside, (128 - 4 * q) % 128, 1)
@@ -107,25 +131,27 @@
     lane = lane_ids((owners, 128))
     r0 = 0.25 * (turn_ref[pl.ds(0, owners, stride=4), :] + turn_ref[pl.ds(1, owners, stride=4), :])
     r1 = 0.25 * (turn_ref[pl.ds(2, owners, stride=4), :] + turn_ref[pl.ds(3, owners, stride=4), :])
-    half = owners // 2
     for c1, out in enumerate((
         jnp.where(lane < 64, r0, pltpu.roll(r1, 64, 1)),
         jnp.where(lane < 64, pltpu.roll(r0, 64, 1), r1),
     )):
-        send_ref[pl.ds(c1, half, stride=2), :] = out[half:]
-        send_ref[pl.ds(2 * half + c1, half, stride=2), :] = out[:half]
+        turn_ref[c1 * owners : c1 * owners + owners, :] = out
+    rest = owners - master
+    for c1 in range(2):
+        at = c1 * owners
+        send_ref[pl.ds(c1, rest, stride=2), :] = turn_ref[at + master : at + owners, :]
+        send_ref[pl.ds(2 * rest + c1, master, stride=2), :] = turn_ref[at : at + master, :]
 
 
 def rebuild_kernel(got_ref, out_ref, wide_ref):
-    level1 = got_ref[...]
+    level1 = pltpu.roll(got_ref[...], 2 * master, 0)
     total = level1 + pltpu.roll(level1, 64, 1)
     coarse = 0.25 * (total + pltpu.roll(total, 32, 1))
     blend = coarse + 0.5 * (level1 - coarse)
-    blend = jnp.concatenate([blend[64:], blend[:64]], axis=0)
-    odd = pltpu.roll(blend, 96, 1)
+    shifted = pltpu.roll(blend, 96, 1)
     for d in range(2):
         wide_ref[pl.ds(d, 128, stride=4), :] = blend
-        wide_ref[pl.ds(2 + d, 128, stride=4), :] = odd
+        wide_ref[pl.ds(2 + d, 128, stride=4), :] = shifted
     for t in range(4):
         turned = wide_ref[128 * t : 128 * t + 128, :].T
         for r in range(2):
@@ -134,12 +160,13 @@
                 out_ref[pl.ds(4 * t + 2 * r + d, 32, stride=16), :] = part
 
 
-def call(kernel, out_shape, scratch=()):
+def call(kernel, out_shape, scratch=(), sems=(), limit=32 * 1024 * 1024, **kw):
     return pl.pallas_call(
         kernel,
         out_shape=out_shape,
-        scratch_shapes=[pltpu.VMEM(s, f32) for s in scratch],
-        compiler_params=pltpu.CompilerParams(vmem_limit_bytes=32 * 1024 * 1024),
+        scratch_shapes=[pltpu.VMEM(s, f32) for s in scratch] + [pltpu.SemaphoreType.DMA(s) for s in sems],
+        compiler_params=pltpu.CompilerParams(vmem_limit_bytes=limit),
+        **kw,
     )
 
 
@@ -147,25 +174,30 @@
     return jax.ShapeDtypeStruct(dims, f32)
 
 
-def ring(axis, by):
+def pairs(axis, first):
     size = lax.axis_size(axis)
-    return [(i, (i + by) % size) for i in range(size)]
+    found = [(i % size, (i + 1) % size) for i in range(first, size, 2)]
+    return found + [(j, i) for i, j in found]
 
 
 def body(u, v):
-    column_halo = shape(2, planes, 2, rows)
-    first, last = call(slice_kernel, (column_halo, column_halo))(u, v)
-    before = lax.ppermute(last, "gy", ring("gy", 1))
-    after = lax.ppermute(first, "gy", ring("gy", -1))
-    edge = call(edge_kernel, shape(16, 128), [(2 * planes, 2, 16, 128)])(u, v, before, after)
-    left = lax.ppermute(edge, "gx", ring("gx", 1))
-    right = lax.ppermute(edge, "gx", ring("gx", -1))
     brick = shape(planes, cols, rows)
+    halo = pltpu.VMEM((2, planes, 2, rows), f32)
+    one, two = call(
+        slice_kernel, (halo, halo), [(planes, cols, rows)] * 2, [(2, 2)], limit=large,
+        in_specs=[pl.BlockSpec(memory_space=pltpu.HBM)] * 2,
+    )(u, v)
+    two = lax.ppermute(two, "gy", pairs("gy", 1))
+    one = lax.ppermute(one, "gy", pairs("gy", 0))
+    edge = call(edge_kernel, shape(16, 128), [(2 * planes, 2, 16, 128)])(u, v, one, two)
+    far = lax.ppermute(edge, "gx", pairs("gx", 1))
+    near = lax.ppermute(edge, "gx", pairs("gx", 0))
+    inside = pltpu.VMEM((planes, cols, rows), f32)
     padded = (2, planes, 16, rows + 128)
     un, vn, send = call(
         step_kernel, (brick, brick, shape(128, 128)), [padded, padded, (2, 256, 128), (rows, 128)]
-    )(u, v, before, after, left, right)
-    order = [(i + owners // 2) % owners for i in range(owners)]
+    )(u, v, one, two, near, far)
+    order = [(i + master) % owners for i in range(owners)]
     got = lax.all_to_all(
         send.reshape(owners, 2, 128), "gy", 0, 0, tiled=True, axis_index_groups=[order]
     )

time: 73.4 us -> 70.4 us (0.959)
  the two profiles are of different devices: /device:TPU:32 before, /device:TPU:24 now
where the time goes in v2:
time: 70.4 us; the launch traced here: 70.1 us
  blocking collectives  48.2 us (68%)
  starting transfers between devices  13.5 us (19%)
  Pallas kernels  3.81 us (5%)
  waiting for transfers between devices  3.79 us (5%)
    all_to_all x1, blocking collectives, body(): lax.all_to_all(send.reshape(owners, 2, 128), 'gy', 0, 0, tiled=True, axis...  48.2 us
    ppermute x1, starting transfers between devices, body(): two = lax.ppermute(two, 'gy', pairs('gy', 1))  5.56 us
    ppermute x1, starting transfers between devices, body(): one = lax.ppermute(one, 'gy', pairs('gy', 0))  3.14 us
    ppermute x1, waiting for transfers between devices, body(): two = lax.ppermute(two, 'gy', pairs('gy', 1))  2.99 us
    ppermute x1, starting transfers between devices, body(): near = lax.ppermute(edge, 'gx', pairs('gx', 0))  2.91 us
    ppermute x1, starting transfers between devices, body(): far = lax.ppermute(edge, 'gx', pairs('gx', 1))  1.92 us
    pallas_call x1, Pallas kernels, body(): call(step_kernel, (brick, brick, shape(128, 128)), [padded, padded, (2, 2...  1.54 us
  transfers between devices with their start and end apart: 4, of which 3 were waited for; matrix products, arithmetic and copies ran while one was open for 0% of the time, Pallas kernels for 0%

profile of v2, /device:TPU:24, one launch (start us, length us, event | category | flops | bytes accessed | tf_op | source)
XLA Modules:
  0.0 70.1 jit_solution(9145366279479453203)
XLA Ops:
  0.6 0.0 copy-start.1
  0.6 0.0 copy-start
  0.6 1.0 %shard_map.49 = (f32[2,16,2,256]{3,2,1,0:T(2,128)S(1)}, f32[2,16,2,256]{3,2,1,0:T(2,128)S(1)}) custom-call(f32[16,8,256]{2,1,0:T(8,128)} %u_ref.3, f32[16,8,256]{2,1,0:T(8,128)} %v_ref.3), custom_call_target="tpu_custom_call" | custom-call | tf_op jit(solution)/shard_map/pallas_call | solution.py:186
  1.7 3.1 %collective-permute-start = (f32[2,16,2,256]{3,2,1,0:T(2,128)S(1)}, f32[2,16,2,256]{3,2,1,0:T(2,128)S(1)}, u32[]{:S(2)}, u32[]{:S(2)}) collective-permute-start(f32[2,16,2,256]{3,2,1,0:T(2,128)S(1)} %get-tuple-element.8), channel_id=1, source_target_pairs={{0,1},{2,3},{4,5},{6,7},{8,9},{10,11},{12,13},{14,15},{16,17},{18,... | collective-permute-start | bytes 196616 | tf_op jit(solution)/shard_map/ppermute | solution.py:191
  4.8 5.6 %collective-permute-start.1 = (f32[2,16,2,256]{3,2,1,0:T(2,128)S(1)}, f32[2,16,2,256]{3,2,1,0:T(2,128)S(1)}, u32[]{:S(2)}, u32[]{:S(2)}) collective-permute-start(f32[2,16,2,256]{3,2,1,0:T(2,128)S(1)} %get-tuple-element.9), channel_id=1, source_target_pairs={{1,2},{3,4},{5,6},{7,8},{9,10},{11,12},{13,14},{15,16},{17,18},{19... | collective-permute-start | bytes 196616 | tf_op jit(solution)/shard_map/ppermute | solution.py:190
  10.4 0.0 collective-permute-done.one_ref
  10.4 3.0 %collective-permute-done.1.two_ref = f32[2,16,2,256]{3,2,1,0:T(2,128)S(1)} collective-permute-done((f32[2,16,2,256]{3,2,1,0:T(2,128)S(1)}, f32[2,16,2,256]{3,2,1,0:T(2,128)S(1)}, u32[]{:S(2)}, u32[]{:S(2)}) %collective-permute-start.1) | collective-permute-done | bytes 65568 | tf_op jit(solution)/shard_map/ppermute | solution.py:190
  13.4 0.0 copy-done.1
  13.4 0.0 copy-done
  13.4 0.2 shard_map.50
  13.6 1.9 %collective-permute-start.3 = (f32[16,128]{1,0:T(8,128)S(1)}, f32[16,128]{1,0:T(8,128)S(1)}, u32[]{:S(2)}, u32[]{:S(2)}) collective-permute-start(f32[16,128]{1,0:T(8,128)S(1)} %shard_map.50), channel_id=1, source_target_pairs={{64,128},{192,256},{320,384},{448,512},{576,640},{704,768},{832,89... | collective-permute-start | bytes 24584 | tf_op jit(solution)/shard_map/ppermute | solution.py:193
  15.5 2.9 %collective-permute-start.2 = (f32[16,128]{1,0:T(8,128)S(1)}, f32[16,128]{1,0:T(8,128)S(1)}, u32[]{:S(2)}, u32[]{:S(2)}) collective-permute-start(f32[16,128]{1,0:T(8,128)S(1)} %shard_map.50), channel_id=1, source_target_pairs={{0,64},{128,192},{256,320},{384,448},{512,576},{640,704},{768,832}... | collective-permute-start | bytes 24584 | tf_op jit(solution)/shard_map/ppermute | solution.py:194
  18.4 0.1 collective-permute-done.3.far_ref
  18.5 0.7 collective-permute-done.2.near_ref
  19.2 1.5 %shard_map.51 = (f32[16,8,256]{2,1,0:T(8,128)}, f32[16,8,256]{2,1,0:T(8,128)}, f32[128,128]{1,0:T(8,128)S(1)}) custom-call(f32[16,8,256]{2,1,0:T(8,128)S(1)} %copy-done, f32[16,8,256]{2,1,0:T(8,128)S(1)} %copy-done.1, f32[2,16,2,256]{3,2,1,0:T(2,128)S(1)} %collective-permute-done.one_ref, f32[2,16,2,256]{3,2,1,0:T(2,128)S(1)} %collective-permute-done.1.two_ref, ...), custom_call_target="tpu_custom_call" | custom-call | tf_op jit(solution)/shard_map/pallas_call | solution.py:197
  20.8 48.2 %all_to_all.5 = f32[64,2,128]{2,1,0:T(2,128)S(1)} all-to-all(f32[64,2,128]{2,1,0:T(2,128)S(1)} %bitcast.8), channel_id=1, replica_groups={{37,38,39,40,41,42,43,44,45,46,47,48,49,50,51,52,53,54,55,56,57,58,59,6..., dimensions={0} | all-to-all | bytes 131072 | tf_op jit(solution)/shard_map/all_to_all | solution.py:201
  69.0 1.1 %shard_map.52 = f32[512,128]{1,0:T(8,128)} custom-call(f32[128,128]{1,0:T(8,128)S(1)} %bitcast.7), custom_call_target="tpu_custom_call" | custom-call | tf_op jit(solution)/shard_map/pallas_call | solution.py:204
Async XLA Ops:
  0.6 12.8 %copy-start.1 = (f32[16,8,256]{2,1,0:T(8,128)S(1)}, f32[16,8,256]{2,1,0:T(8,128)}, u32[]{:S(2)}) copy-start(f32[16,8,256]{2,1,0:T(8,128)} %v_ref.3) | copy-start | bytes 393220
  0.6 12.8 %copy-start = (f32[16,8,256]{2,1,0:T(8,128)S(1)}, f32[16,8,256]{2,1,0:T(8,128)}, u32[]{:S(2)}) copy-start(f32[16,8,256]{2,1,0:T(8,128)} %u_ref.3) | copy-start | bytes 393220
  1.7 8.7 %collective-permute-start = (f32[2,16,2,256]{3,2,1,0:T(2,128)S(1)}, f32[2,16,2,256]{3,2,1,0:T(2,128)S(1)}, u32[]{:S(2)}, u32[]{:S(2)}) collective-permute-start(f32[2,16,2,256]{3,2,1,0:T(2,128)S(1)} %get-tuple-element.8), channel_id=1, source_target_pairs={{0,1},{2,3},{4,5},{6,7},{8,9},{10,11},{12,13},{14,15},{16,17},{18,... | collective-permute-start | bytes 196616 | tf_op jit(solution)/shard_map/ppermute | solution.py:191
  4.8 8.6 %collective-permute-start.1 = (f32[2,16,2,256]{3,2,1,0:T(2,128)S(1)}, f32[2,16,2,256]{3,2,1,0:T(2,128)S(1)}, u32[]{:S(2)}, u32[]{:S(2)}) collective-permute-start(f32[2,16,2,256]{3,2,1,0:T(2,128)S(1)} %get-tuple-element.9), channel_id=1, source_target_pairs={{1,2},{3,4},{5,6},{7,8},{9,10},{11,12},{13,14},{15,16},{17,18},{19... | collective-permute-start | bytes 196616 | tf_op jit(solution)/shard_map/ppermute | solution.py:190
  13.6 5.0 %collective-permute-start.3 = (f32[16,128]{1,0:T(8,128)S(1)}, f32[16,128]{1,0:T(8,128)S(1)}, u32[]{:S(2)}, u32[]{:S(2)}) collective-permute-start(f32[16,128]{1,0:T(8,128)S(1)} %shard_map.50), channel_id=1, source_target_pairs={{64,128},{192,256},{320,384},{448,512},{576,640},{704,768},{832,89... | collective-permute-start | bytes 24584 | tf_op jit(solution)/shard_map/ppermute | solution.py:193
  15.5 3.7 %collective-permute-start.2 = (f32[16,128]{1,0:T(8,128)S(1)}, f32[16,128]{1,0:T(8,128)S(1)}, u32[]{:S(2)}, u32[]{:S(2)}) collective-permute-start(f32[16,128]{1,0:T(8,128)S(1)} %shard_map.50), channel_id=1, source_target_pairs={{0,64},{128,192},{256,320},{384,448},{512,576},{640,704},{768,832}... | collective-permute-start | bytes 24584 | tf_op jit(solution)/shard_map/ppermute | solution.py:194

commit v3 on v2

--- a/solution.py
+++ b/solution.py
@@ -25,40 +25,33 @@
     return lax.axis_index(axis) % 2 == 1
 
 
-def slice_kernel(u_hbm, v_hbm, one_ref, two_ref, u_ref, v_ref, sems):
-    part = planes // 2
+def slice_kernel(u_hbm, v_hbm, first_ref, u_ref, v_ref, sems):
+    part, some = planes // 2, pl.ds(0, 4)
     copies = []
     for f, (src, dst) in enumerate(((u_hbm, u_ref), (v_hbm, v_ref))):
         for h in range(2):
             at = pl.ds(h * part, part)
-            copies.append((f, h, pltpu.make_async_copy(src.at[at], dst.at[at], sems.at[f, h])))
-    for _, _, copy in copies:
-        copy.start()
-    second = odd("gy")
+            copy = pltpu.make_async_copy(src.at[at, some], dst.at[at, some], sems.at[f, h])
+            copy.start()
+            copies.append((f, h, copy))
     for f, h, copy in copies:
         copy.wait()
         at = slice(h * part, h * part + part)
-        ref = (u_ref, v_ref)[f]
-        first, last = ref[at, 0:2, :], ref[at, cols - 2 : cols, :]
-        one_ref[f, at] = jnp.where(second, first, last)
-        two_ref[f, at] = jnp.where(second, last, first)
-
-
-def edge_kernel(u_ref, v_ref, one_ref, two_ref, edge_ref, pad_ref):
+        first_ref[f, at] = (u_ref, v_ref)[f][at, 0:4, :]
+
+
+def edge_kernel(u_ref, v_ref, next_ref, edge_ref, pad_ref):
     lane = lane_ids((16, 128))
     low = lane < 64
     here = (lane < 2) | (lane >= 126)
     packed = jnp.zeros((16, 128), f32)
-    second = odd("gy")
     for f, ref in enumerate((u_ref, v_ref)):
         for p in range(planes):
-            one, two = one_ref[f, p], two_ref[f, p]
-            after, before = jnp.where(second, two, one), jnp.where(second, one, two)
             q = f * planes + p
             for t, lanes in enumerate((slice(0, 128), slice(rows - 128, rows))):
-                pad_ref[q, t, 0:8, :] = ref[p, :, lanes]
-                pad_ref[q, t, 8:10, :] = after[:, lanes]
-                pad_ref[q, t, 14:16, :] = before[:, lanes]
+                pad_ref[q, t, 0:6, :] = ref[p, 2:8, lanes]
+                pad_ref[q, t, 6:10, :] = next_ref[f, p, :, lanes]
+                pad_ref[q, t, 14:16, :] = ref[p, 0:2, lanes]
     for q in range(2 * planes):
         both = jnp.where(low, pad_ref[q, 0], pad_ref[q, 1])
         moved = pltpu.roll(jnp.where(here, both, 0.0), 4 * q % 128, 1)
@@ -83,18 +76,16 @@
 
 
 def step_kernel(
-    u_ref, v_ref, one_ref, two_ref, near_ref, far_ref,
-    un_ref, vn_ref, send_ref, pad_ref, mid_ref, done_ref, turn_ref,
+    u_ref, v_ref, next_ref, near_ref, far_ref,
+    un_ref, vn_ref, back_ref, send_ref, pad_ref, mid_ref, done_ref, turn_ref,
 ):
     right = lane_ids((16, 128)) % 4 < 2
     beside = jnp.where(right != odd("gx"), near_ref[...], far_ref[...])
-    second = odd("gy")
     for f, ref in enumerate((u_ref, v_ref)):
         pad_ref[f, :, 10:14, 0:rows] = jnp.zeros((planes, 4, rows), f32)
-        pad_ref[f, :, 0:8, 0:rows] = ref[...]
-        one, two = one_ref[f], two_ref[f]
-        pad_ref[f, :, 8:10, 0:rows] = jnp.where(second, two, one)
-        pad_ref[f, :, 14:16, 0:rows] = jnp.where(second, one, two)
+        pad_ref[f, :, 0:6, 0:rows] = ref[:, 2:8, :]
+        pad_ref[f, :, 6:10, 0:rows] = next_ref[f]
+        pad_ref[f, :, 14:16, 0:rows] = ref[:, 0:2, :]
         for p in range(planes):
             q = f * planes + p
             pad_ref[f, p, :, rows : rows + 128] = pltpu.roll(beside, (128 - 4 * q) % 128, 1)
@@ -116,6 +107,7 @@
         new_u, new_v = react(u, v, spread_u, spread_v)
         for f, (ref, new) in enumerate(((un_ref, new_u), (vn_ref, new_v))):
             ref[p] = new[0:8, 0:rows]
+            back_ref[f, p] = new[6:8, 0:rows]
             at = 8 * (f * planes + p)
             for t in range(2):
                 done_ref[t, at : at + 8, :] = new[0:8, 128 * t : 128 * t + 128]
@@ -143,8 +135,16 @@
         send_ref[pl.ds(2 * rest + c1, master, stride=2), :] = turn_ref[at : at + master, :]
 
 
+def join_kernel(un_ref, vn_ref, back_ref, u_out, v_out):
+    for f, (ref, out) in enumerate(((un_ref, u_out), (vn_ref, v_out))):
+        out[:, 0:2, :] = back_ref[f]
+        out[:, 2:8, :] = ref[:, 0:6, :]
+
+
 def rebuild_kernel(got_ref, out_ref, wide_ref):
-    level1 = pltpu.roll(got_ref[...], 2 * master, 0)
+    got = pltpu.roll(got_ref[...], 2 * master, 0)
+    even = lane_ids((128, 128)) % 64 < 32
+    level1 = jnp.where(even, pltpu.roll(pltpu.roll(got, 1, 0), 96, 1), pltpu.roll(got, 32, 1))
     total = level1 + pltpu.roll(level1, 64, 1)
     coarse = 0.25 * (total + pltpu.roll(total, 32, 1))
     blend = coarse + 0.5 * (level1 - coarse)
@@ -174,6 +174,11 @@
     return jax.ShapeDtypeStruct(dims, f32)
 
 
+def ring(axis, by):
+    size = lax.axis_size(axis)
+    return [(i, (i + by) % size) for i in range(size)]
+
+
 def pairs(axis, first):
     size = lax.axis_size(axis)
     found = [(i % size, (i + 1) % size) for i in range(first, size, 2)]
@@ -182,21 +187,22 @@
 
 def body(u, v):
     brick = shape(planes, cols, rows)
-    halo = pltpu.VMEM((2, planes, 2, rows), f32)
-    one, two = call(
-        slice_kernel, (halo, halo), [(planes, cols, rows)] * 2, [(2, 2)], limit=large,
-        in_specs=[pl.BlockSpec(memory_space=pltpu.HBM)] * 2,
+    inside = pltpu.VMEM((planes, cols, rows), f32)
+    first = call(
+        slice_kernel, pltpu.VMEM((2, planes, 4, rows), f32), [(planes, cols, rows)] * 2, [(2, 2)],
+        limit=large, in_specs=[pl.BlockSpec(memory_space=pltpu.HBM)] * 2,
     )(u, v)
-    two = lax.ppermute(two, "gy", pairs("gy", 1))
-    one = lax.ppermute(one, "gy", pairs("gy", 0))
-    edge = call(edge_kernel, shape(16, 128), [(2 * planes, 2, 16, 128)])(u, v, one, two)
+    after = lax.ppermute(first, "gy", ring("gy", -1))
+    edge = call(edge_kernel, shape(16, 128), [(2 * planes, 2, 16, 128)])(u, v, after)
     far = lax.ppermute(edge, "gx", pairs("gx", 1))
     near = lax.ppermute(edge, "gx", pairs("gx", 0))
-    inside = pltpu.VMEM((planes, cols, rows), f32)
     padded = (2, planes, 16, rows + 128)
-    un, vn, send = call(
-        step_kernel, (brick, brick, shape(128, 128)), [padded, padded, (2, 256, 128), (rows, 128)]
-    )(u, v, one, two, near, far)
+    un, vn, back, send = call(
+        step_kernel, (inside, inside, shape(2, planes, 2, rows), shape(128, 128)),
+        [padded, padded, (2, 256, 128), (rows, 128)],
+    )(u, v, after, near, far)
+    back = lax.ppermute(back, "gy", ring("gy", 1))
+    un, vn = call(join_kernel, (brick, brick))(un, vn, back)
     order = [(i + master) % owners for i in range(owners)]
     got = lax.all_to_all(
         send.reshape(owners, 2, 128), "gy", 0, 0, tiled=True, axis_index_groups=[order]

time: 70.4 us -> 69.9 us (level)
  the two profiles are of different devices: /device:TPU:24 before, /device:TPU:1 now
where the time goes in v3:
time: 69.9 us; the launch traced here: 69.6 us
  starting transfers between devices  54.8 us (78%)
  waiting for transfers between devices  9.48 us (14%)
  Pallas kernels  4.67 us (7%)
  between operations  0.71 us (1%)
    all_to_all x1, starting transfers between devices, body(): lax.all_to_all(send.reshape(owners, 2, 128), 'gy', 0, 0, tiled=True, axis...  23.9 us
    ppermute x1, starting transfers between devices, body(): after = lax.ppermute(first, 'gy', ring('gy', -1))  21.9 us
    ppermute x1, waiting for transfers between devices, body(): back = lax.ppermute(back, 'gy', ring('gy', 1))  6.53 us
    ppermute x1, starting transfers between devices, body(): far = lax.ppermute(edge, 'gx', pairs('gx', 1))  3.73 us
    ppermute x1, starting transfers between devices, body(): near = lax.ppermute(edge, 'gx', pairs('gx', 0))  3.07 us
    ppermute x1, starting transfers between devices, body(): back = lax.ppermute(back, 'gy', ring('gy', 1))  2.2 us
    ppermute x1, waiting for transfers between devices, body(): after = lax.ppermute(first, 'gy', ring('gy', -1))  2.14 us
    pallas_call x1, Pallas kernels, body(): call(step_kernel, (inside, inside, shape(2, planes, 2, rows), shape(128,...  1.71 us
  transfers between devices with their start and end apart: 5, of which 3 were waited for; matrix products, arithmetic and copies ran while one was open for 0% of the time, Pallas kernels for 1%

profile of v3, /device:TPU:1, one launch (start us, length us, event | category | flops | bytes accessed | tf_op | source)
XLA Modules:
  0.0 69.6 jit_solution(3689512357820356129)
XLA Ops:
  0.6 0.0 copy-start.1
  0.6 0.0 copy-start
  0.6 0.9 %shard_map.49 = f32[2,16,4,256]{3,2,1,0:T(4,128)S(1)} custom-call(f32[16,8,256]{2,1,0:T(8,128)} %u_ref.3, f32[16,8,256]{2,1,0:T(8,128)} %v_ref.3), custom_call_target="tpu_custom_call" | custom-call | tf_op jit(solution)/shard_map/pallas_call | solution.py:191
  1.5 21.9 %collective-permute-start = (f32[2,16,4,256]{3,2,1,0:T(4,128)S(1)}, f32[2,16,4,256]{3,2,1,0:T(4,128)S(1)}, u32[]{:S(2)}, u32[]{:S(2)}) collective-permute-start(f32[2,16,4,256]{3,2,1,0:T(4,128)S(1)} %shard_map.49), channel_id=1, source_target_pairs={{0,63},{1,0},{2,1},{3,2},{4,3},{5,4},{6,5},{7,6},{8,7},{9,8},{10,9... | collective-permute-start | bytes 393224 | tf_op jit(solution)/shard_map/ppermute | solution.py:195
  23.4 2.1 %collective-permute-done.next_ref = f32[2,16,4,256]{3,2,1,0:T(4,128)S(1)} collective-permute-done((f32[2,16,4,256]{3,2,1,0:T(4,128)S(1)}, f32[2,16,4,256]{3,2,1,0:T(4,128)S(1)}, u32[]{:S(2)}, u32[]{:S(2)}) %collective-permute-start) | collective-permute-done | bytes 131104 | tf_op jit(solution)/shard_map/ppermute | solution.py:195
  25.6 0.0 copy-done.1
  25.6 0.0 copy-done
  25.6 0.2 shard_map.50
  25.7 3.7 %collective-permute-start.2 = (f32[16,128]{1,0:T(8,128)S(1)}, f32[16,128]{1,0:T(8,128)S(1)}, u32[]{:S(2)}, u32[]{:S(2)}) collective-permute-start(f32[16,128]{1,0:T(8,128)S(1)} %shard_map.50), channel_id=1, source_target_pairs={{64,128},{192,256},{320,384},{448,512},{576,640},{704,768},{832,89... | collective-permute-start | bytes 24584 | tf_op jit(solution)/shard_map/ppermute | solution.py:197
  29.5 3.1 %collective-permute-start.1 = (f32[16,128]{1,0:T(8,128)S(1)}, f32[16,128]{1,0:T(8,128)S(1)}, u32[]{:S(2)}, u32[]{:S(2)}) collective-permute-start(f32[16,128]{1,0:T(8,128)S(1)} %shard_map.50), channel_id=1, source_target_pairs={{0,64},{128,192},{256,320},{384,448},{512,576},{640,704},{768,832}... | collective-permute-start | bytes 24584 | tf_op jit(solution)/shard_map/ppermute | solution.py:198
  32.5 0.0 collective-permute-done.2.far_ref
  32.6 0.8 %collective-permute-done.1.near_ref = f32[16,128]{1,0:T(8,128)S(1)} collective-permute-done((f32[16,128]{1,0:T(8,128)S(1)}, f32[16,128]{1,0:T(8,128)S(1)}, u32[]{:S(2)}, u32[]{:S(2)}) %collective-permute-start.1) | collective-permute-done | bytes 8224 | tf_op jit(solution)/shard_map/ppermute | solution.py:198
  33.3 1.7 %shard_map.51 = (f32[16,8,256]{2,1,0:T(8,128)S(1)}, f32[16,8,256]{2,1,0:T(8,128)S(1)}, f32[2,16,2,256]{3,2,1,0:T(2,128)S(1)}, f32[128,128]{1,0:T(8,128)}) custom-call(f32[16,8,256]{2,1,0:T(8,128)S(1)} %copy-done, f32[16,8,256]{2,1,0:T(8,128)S(1)} %copy-done.1, f32[2,16,4,256]{3,2,1,0:T(4,128)S(1)} %collective-permute-done.next_ref, ...), custom_call_target="tpu_custom_call" | custom-call | tf_op jit(solution)/shard_map/pallas_call | solution.py:200
  35.1 23.9 %all-to-all-start = ((f32[64,2,128]{2,1,0:T(2,128)}), f32[64,2,128]{2,1,0:T(2,128)S(1)}, u32[]{:S(2)}, u32[]{:S(2)}) async-start(f32[64,2,128]{2,1,0:T(2,128)} %bitcast), calls=%async_computation | async-start | bytes 131072 | tf_op jit(solution)/shard_map/all_to_all | solution.py:207
  59.0 2.2 %collective-permute-start.3 = (f32[2,16,2,256]{3,2,1,0:T(2,128)S(1)}, f32[2,16,2,256]{3,2,1,0:T(2,128)S(1)}, u32[]{:S(2)}, u32[]{:S(2)}) collective-permute-start(f32[2,16,2,256]{3,2,1,0:T(2,128)S(1)} %get-tuple-element.11), channel_id=1, source_target_pairs={{0,1},{1,2},{2,3},{3,4},{4,5},{5,6},{6,7},{7,8},{8,9},{9,10},{10,1... | collective-permute-start | bytes 196616 | tf_op jit(solution)/shard_map/ppermute | solution.py:204
  61.2 6.5 %collective-permute-done.3.back_ref = f32[2,16,2,256]{3,2,1,0:T(2,128)S(1)} collective-permute-done((f32[2,16,2,256]{3,2,1,0:T(2,128)S(1)}, f32[2,16,2,256]{3,2,1,0:T(2,128)S(1)}, u32[]{:S(2)}, u32[]{:S(2)}) %collective-permute-start.3) | collective-permute-done | bytes 65568 | tf_op jit(solution)/shard_map/ppermute | solution.py:204
  67.7 0.8 %shard_map.52 = (f32[16,8,256]{2,1,0:T(8,128)}, f32[16,8,256]{2,1,0:T(8,128)}) custom-call(f32[16,8,256]{2,1,0:T(8,128)S(1)} %get-tuple-element.9.un_ref, f32[16,8,256]{2,1,0:T(8,128)S(1)} %get-tuple-element.10.vn_ref, f32[2,16,2,256]{3,2,1,0:T(2,128)S(1)} %collective-permute-done.3.back_ref), custom_call_target="tpu_custom_call" | custom-call | tf_op jit(solution)/shard_map/pallas_call | solution.py:205
  68.5 0.0 all-to-all-done
  68.5 1.2 %shard_map.53 = f32[512,128]{1,0:T(8,128)} custom-call(f32[128,128]{1,0:T(8,128)S(1)} %bitcast.7), custom_call_target="tpu_custom_call" | custom-call | tf_op jit(solution)/shard_map/pallas_call | solution.py:210
Async XLA Ops:
  0.6 24.9 %copy-start.1 = (f32[16,8,256]{2,1,0:T(8,128)S(1)}, f32[16,8,256]{2,1,0:T(8,128)}, u32[]{:S(2)}) copy-start(f32[16,8,256]{2,1,0:T(8,128)} %v_ref.3) | copy-start | bytes 393220
  0.6 24.9 %copy-start = (f32[16,8,256]{2,1,0:T(8,128)S(1)}, f32[16,8,256]{2,1,0:T(8,128)}, u32[]{:S(2)}) copy-start(f32[16,8,256]{2,1,0:T(8,128)} %u_ref.3) | copy-start | bytes 393220
  1.5 24.0 %collective-permute-start = (f32[2,16,4,256]{3,2,1,0:T(4,128)S(1)}, f32[2,16,4,256]{3,2,1,0:T(4,128)S(1)}, u32[]{:S(2)}, u32[]{:S(2)}) collective-permute-start(f32[2,16,4,256]{3,2,1,0:T(4,128)S(1)} %shard_map.49), channel_id=1, source_target_pairs={{0,63},{1,0},{2,1},{3,2},{4,3},{5,4},{6,5},{7,6},{8,7},{9,8},{10,9... | collective-permute-start | bytes 393224 | tf_op jit(solution)/shard_map/ppermute | solution.py:195
  25.7 6.8 %collective-permute-start.2 = (f32[16,128]{1,0:T(8,128)S(1)}, f32[16,128]{1,0:T(8,128)S(1)}, u32[]{:S(2)}, u32[]{:S(2)}) collective-permute-start(f32[16,128]{1,0:T(8,128)S(1)} %shard_map.50), channel_id=1, source_target_pairs={{64,128},{192,256},{320,384},{448,512},{576,640},{704,768},{832,89... | collective-permute-start | bytes 24584 | tf_op jit(solution)/shard_map/ppermute | solution.py:197
  29.5 3.9 %collective-permute-start.1 = (f32[16,128]{1,0:T(8,128)S(1)}, f32[16,128]{1,0:T(8,128)S(1)}, u32[]{:S(2)}, u32[]{:S(2)}) collective-permute-start(f32[16,128]{1,0:T(8,128)S(1)} %shard_map.50), channel_id=1, source_target_pairs={{0,64},{128,192},{256,320},{384,448},{512,576},{640,704},{768,832}... | collective-permute-start | bytes 24584 | tf_op jit(solution)/shard_map/ppermute | solution.py:198
  35.1 33.4 %all-to-all-start = ((f32[64,2,128]{2,1,0:T(2,128)}), f32[64,2,128]{2,1,0:T(2,128)S(1)}, u32[]{:S(2)}, u32[]{:S(2)}) async-start(f32[64,2,128]{2,1,0:T(2,128)} %bitcast), calls=%async_computation | async-start | bytes 131072 | tf_op jit(solution)/shard_map/all_to_all | solution.py:207
  59.0 8.7 %collective-permute-start.3 = (f32[2,16,2,256]{3,2,1,0:T(2,128)S(1)}, f32[2,16,2,256]{3,2,1,0:T(2,128)S(1)}, u32[]{:S(2)}, u32[]{:S(2)}) collective-permute-start(f32[2,16,2,256]{3,2,1,0:T(2,128)S(1)} %get-tuple-element.11), channel_id=1, source_target_pairs={{0,1},{1,2},{2,3},{3,4},{4,5},{5,6},{6,7},{7,8},{8,9},{9,10},{10,1... | collective-permute-start | bytes 196616 | tf_op jit(solution)/shard_map/ppermute | solution.py:204

commit v4 on v3

--- a/solution.py
+++ b/solution.py
@@ -13,7 +13,7 @@
 planes, cols, rows = 16, 8, 256
 owners = 64
 large = 56 * 1024 * 1024
-master = 37
+master = 43
 f32 = jnp.float32
 
 

time: 69.9 us -> 67.9 us (0.971)
  the two profiles are of different devices: /device:TPU:1 before, /device:TPU:24 now
where the time goes in v4:
time: 67.9 us; the launch traced here: 67.2 us
  starting transfers between devices  46.3 us (68%)
  waiting for transfers between devices  15.5 us (23%)
  Pallas kernels  4.67 us (7%)
  between operations  0.71 us (1%)
    all_to_all x1, starting transfers between devices, body(): lax.all_to_all(send.reshape(owners, 2, 128), 'gy', 0, 0, tiled=True, axis...  31.8 us
    ppermute x1, waiting for transfers between devices, body(): after = lax.ppermute(first, 'gy', ring('gy', -1))  6.38 us
    all_to_all x1, waiting for transfers between devices, body(): lax.all_to_all(send.reshape(owners, 2, 128), 'gy', 0, 0, tiled=True, axis...  6.38 us
    ppermute x1, starting transfers between devices, body(): back = lax.ppermute(back, 'gy', ring('gy', 1))  5.78 us
    ppermute x1, starting transfers between devices, body(): near = lax.ppermute(edge, 'gx', pairs('gx', 0))  3.68 us
    ppermute x1, starting transfers between devices, body(): after = lax.ppermute(first, 'gy', ring('gy', -1))  3.14 us
    ppermute x1, starting transfers between devices, body(): far = lax.ppermute(edge, 'gx', pairs('gx', 1))  1.91 us
    ppermute x1, waiting for transfers between devices, body(): back = lax.ppermute(back, 'gy', ring('gy', 1))  1.9 us
  transfers between devices with their start and end apart: 5, of which 4 were waited for; matrix products, arithmetic and copies ran while one was open for 0% of the time, Pallas kernels for 1%

profile of v4, /device:TPU:24, one launch (start us, length us, event | category | flops | bytes accessed | tf_op | source)
XLA Modules:
  0.0 67.2 jit_solution(14977062838038834551)
XLA Ops:
  0.6 0.0 copy-start.1
  0.6 0.0 copy-start
  0.6 0.9 %shard_map.49 = f32[2,16,4,256]{3,2,1,0:T(4,128)S(1)} custom-call(f32[16,8,256]{2,1,0:T(8,128)} %u_ref.3, f32[16,8,256]{2,1,0:T(8,128)} %v_ref.3), custom_call_target="tpu_custom_call" | custom-call | tf_op jit(solution)/shard_map/pallas_call | solution.py:191
  1.5 3.1 %collective-permute-start = (f32[2,16,4,256]{3,2,1,0:T(4,128)S(1)}, f32[2,16,4,256]{3,2,1,0:T(4,128)S(1)}, u32[]{:S(2)}, u32[]{:S(2)}) collective-permute-start(f32[2,16,4,256]{3,2,1,0:T(4,128)S(1)} %shard_map.49), channel_id=1, source_target_pairs={{0,63},{1,0},{2,1},{3,2},{4,3},{5,4},{6,5},{7,6},{8,7},{9,8},{10,9... | collective-permute-start | bytes 393224 | tf_op jit(solution)/shard_map/ppermute | solution.py:195
  4.7 6.4 %collective-permute-done.next_ref = f32[2,16,4,256]{3,2,1,0:T(4,128)S(1)} collective-permute-done((f32[2,16,4,256]{3,2,1,0:T(4,128)S(1)}, f32[2,16,4,256]{3,2,1,0:T(4,128)S(1)}, u32[]{:S(2)}, u32[]{:S(2)}) %collective-permute-start) | collective-permute-done | bytes 131104 | tf_op jit(solution)/shard_map/ppermute | solution.py:195
  11.1 0.0 copy-done.1
  11.1 0.0 copy-done
  11.1 0.2 shard_map.50
  11.3 1.9 %collective-permute-start.2 = (f32[16,128]{1,0:T(8,128)S(1)}, f32[16,128]{1,0:T(8,128)S(1)}, u32[]{:S(2)}, u32[]{:S(2)}) collective-permute-start(f32[16,128]{1,0:T(8,128)S(1)} %shard_map.50), channel_id=1, source_target_pairs={{64,128},{192,256},{320,384},{448,512},{576,640},{704,768},{832,89... | collective-permute-start | bytes 24584 | tf_op jit(solution)/shard_map/ppermute | solution.py:197
  13.2 3.7 %collective-permute-start.1 = (f32[16,128]{1,0:T(8,128)S(1)}, f32[16,128]{1,0:T(8,128)S(1)}, u32[]{:S(2)}, u32[]{:S(2)}) collective-permute-start(f32[16,128]{1,0:T(8,128)S(1)} %shard_map.50), channel_id=1, source_target_pairs={{0,64},{128,192},{256,320},{384,448},{512,576},{640,704},{768,832}... | collective-permute-start | bytes 24584 | tf_op jit(solution)/shard_map/ppermute | solution.py:198
  16.9 0.0 collective-permute-done.2.far_ref
  16.9 0.8 %collective-permute-done.1.near_ref = f32[16,128]{1,0:T(8,128)S(1)} collective-permute-done((f32[16,128]{1,0:T(8,128)S(1)}, f32[16,128]{1,0:T(8,128)S(1)}, u32[]{:S(2)}, u32[]{:S(2)}) %collective-permute-start.1) | collective-permute-done | bytes 8224 | tf_op jit(solution)/shard_map/ppermute | solution.py:198
  17.7 1.7 %shard_map.51 = (f32[16,8,256]{2,1,0:T(8,128)S(1)}, f32[16,8,256]{2,1,0:T(8,128)S(1)}, f32[2,16,2,256]{3,2,1,0:T(2,128)S(1)}, f32[128,128]{1,0:T(8,128)}) custom-call(f32[16,8,256]{2,1,0:T(8,128)S(1)} %copy-done, f32[16,8,256]{2,1,0:T(8,128)S(1)} %copy-done.1, f32[2,16,4,256]{3,2,1,0:T(4,128)S(1)} %collective-permute-done.next_ref, ...), custom_call_target="tpu_custom_call" | custom-call | tf_op jit(solution)/shard_map/pallas_call | solution.py:200
  19.4 31.8 %all-to-all-start = ((f32[64,2,128]{2,1,0:T(2,128)}), f32[64,2,128]{2,1,0:T(2,128)S(1)}, u32[]{:S(2)}, u32[]{:S(2)}) async-start(f32[64,2,128]{2,1,0:T(2,128)} %bitcast), calls=%async_computation | async-start | bytes 131072 | tf_op jit(solution)/shard_map/all_to_all | solution.py:207
  51.2 5.8 %collective-permute-start.3 = (f32[2,16,2,256]{3,2,1,0:T(2,128)S(1)}, f32[2,16,2,256]{3,2,1,0:T(2,128)S(1)}, u32[]{:S(2)}, u32[]{:S(2)}) collective-permute-start(f32[2,16,2,256]{3,2,1,0:T(2,128)S(1)} %get-tuple-element.11), channel_id=1, source_target_pairs={{0,1},{1,2},{2,3},{3,4},{4,5},{5,6},{6,7},{7,8},{8,9},{9,10},{10,1... | collective-permute-start | bytes 196616 | tf_op jit(solution)/shard_map/ppermute | solution.py:204
  57.0 1.9 %collective-permute-done.3.back_ref = f32[2,16,2,256]{3,2,1,0:T(2,128)S(1)} collective-permute-done((f32[2,16,2,256]{3,2,1,0:T(2,128)S(1)}, f32[2,16,2,256]{3,2,1,0:T(2,128)S(1)}, u32[]{:S(2)}, u32[]{:S(2)}) %collective-permute-start.3) | collective-permute-done | bytes 65568 | tf_op jit(solution)/shard_map/ppermute | solution.py:204
  58.9 0.8 %shard_map.52 = (f32[16,8,256]{2,1,0:T(8,128)}, f32[16,8,256]{2,1,0:T(8,128)}) custom-call(f32[16,8,256]{2,1,0:T(8,128)S(1)} %get-tuple-element.9.un_ref, f32[16,8,256]{2,1,0:T(8,128)S(1)} %get-tuple-element.10.vn_ref, f32[2,16,2,256]{3,2,1,0:T(2,128)S(1)} %collective-permute-done.3.back_ref), custom_call_target="tpu_custom_call" | custom-call | tf_op jit(solution)/shard_map/pallas_call | solution.py:205
  59.6 6.4 %all-to-all-done = f32[64,2,128]{2,1,0:T(2,128)S(1)} async-done(((f32[64,2,128]{2,1,0:T(2,128)}), f32[64,2,128]{2,1,0:T(2,128)S(1)}, u32[]{:S(2)}, u32[]{:S(2)}) %all-to-all-start) | async-done | bytes 65568 | tf_op jit(solution)/shard_map/all_to_all | solution.py:207
  66.0 1.2 %shard_map.53 = f32[512,128]{1,0:T(8,128)} custom-call(f32[128,128]{1,0:T(8,128)S(1)} %bitcast.7), custom_call_target="tpu_custom_call" | custom-call | tf_op jit(solution)/shard_map/pallas_call | solution.py:210
Async XLA Ops:
  0.6 10.4 %copy-start.1 = (f32[16,8,256]{2,1,0:T(8,128)S(1)}, f32[16,8,256]{2,1,0:T(8,128)}, u32[]{:S(2)}) copy-start(f32[16,8,256]{2,1,0:T(8,128)} %v_ref.3) | copy-start | bytes 393220
  0.6 10.4 %copy-start = (f32[16,8,256]{2,1,0:T(8,128)S(1)}, f32[16,8,256]{2,1,0:T(8,128)}, u32[]{:S(2)}) copy-start(f32[16,8,256]{2,1,0:T(8,128)} %u_ref.3) | copy-start | bytes 393220
  1.5 9.5 %collective-permute-start = (f32[2,16,4,256]{3,2,1,0:T(4,128)S(1)}, f32[2,16,4,256]{3,2,1,0:T(4,128)S(1)}, u32[]{:S(2)}, u32[]{:S(2)}) collective-permute-start(f32[2,16,4,256]{3,2,1,0:T(4,128)S(1)} %shard_map.49), channel_id=1, source_target_pairs={{0,63},{1,0},{2,1},{3,2},{4,3},{5,4},{6,5},{7,6},{8,7},{9,8},{10,9... | collective-permute-start | bytes 393224 | tf_op jit(solution)/shard_map/ppermute | solution.py:195
  11.3 5.6 %collective-permute-start.2 = (f32[16,128]{1,0:T(8,128)S(1)}, f32[16,128]{1,0:T(8,128)S(1)}, u32[]{:S(2)}, u32[]{:S(2)}) collective-permute-start(f32[16,128]{1,0:T(8,128)S(1)} %shard_map.50), channel_id=1, source_target_pairs={{64,128},{192,256},{320,384},{448,512},{576,640},{704,768},{832,89... | collective-permute-start | bytes 24584 | tf_op jit(solution)/shard_map/ppermute | solution.py:197
  13.2 4.5 %collective-permute-start.1 = (f32[16,128]{1,0:T(8,128)S(1)}, f32[16,128]{1,0:T(8,128)S(1)}, u32[]{:S(2)}, u32[]{:S(2)}) collective-permute-start(f32[16,128]{1,0:T(8,128)S(1)} %shard_map.50), channel_id=1, source_target_pairs={{0,64},{128,192},{256,320},{384,448},{512,576},{640,704},{768,832}... | collective-permute-start | bytes 24584 | tf_op jit(solution)/shard_map/ppermute | solution.py:198
  19.4 46.6 %all-to-all-start = ((f32[64,2,128]{2,1,0:T(2,128)}), f32[64,2,128]{2,1,0:T(2,128)S(1)}, u32[]{:S(2)}, u32[]{:S(2)}) async-start(f32[64,2,128]{2,1,0:T(2,128)} %bitcast), calls=%async_computation | async-start | bytes 131072 | tf_op jit(solution)/shard_map/all_to_all | solution.py:207
  51.2 7.7 %collective-permute-start.3 = (f32[2,16,2,256]{3,2,1,0:T(2,128)S(1)}, f32[2,16,2,256]{3,2,1,0:T(2,128)S(1)}, u32[]{:S(2)}, u32[]{:S(2)}) collective-permute-start(f32[2,16,2,256]{3,2,1,0:T(2,128)S(1)} %get-tuple-element.11), channel_id=1, source_target_pairs={{0,1},{1,2},{2,3},{3,4},{4,5},{5,6},{6,7},{7,8},{8,9},{9,10},{10,1... | collective-permute-start | bytes 196616 | tf_op jit(solution)/shard_map/ppermute | solution.py:204

commit v5 on v4

--- a/solution.py
+++ b/solution.py
@@ -60,14 +60,6 @@
     edge_ref[...] = jnp.where((row < 10) | (row >= 14), packed, 0.0)
 
 
-def neighbours(x, below, above):
-    n, m = x.shape
-    total = below + above
-    total = total + pltpu.roll(x, 1, 0) + pltpu.roll(x, n - 1, 0)
-    total = total + pltpu.roll(x, 1, 1) + pltpu.roll(x, m - 1, 1)
-    return total - 6.0 * x
-
-
 def react(u, v, spread_u, spread_v):
     reaction = u * v * v
     new_u = u + substrate_diffusion * spread_u - reaction + feed_rate * (1.0 - u)
@@ -75,42 +67,80 @@
     return new_u, new_v
 
 
+def inner_kernel(u_ref, v_ref, next_ref, edge_ref, mid_ref, pad_ref):
+    del edge_ref
+    for f, ref in enumerate((u_ref, v_ref)):
+        pad_ref[f, :, 10:14, :] = jnp.zeros((planes, 4, rows), f32)
+        pad_ref[f, :, 0:6, :] = ref[:, 2:8, :]
+        pad_ref[f, :, 6:10, :] = next_ref[f]
+        pad_ref[f, :, 14:16, :] = ref[:, 0:2, :]
+    lane = lane_ids((16, rows))
+    for p in range(planes):
+        spreads = []
+        for f in range(2):
+            x = pad_ref[f, p]
+            total = pad_ref[f, (p - 1) % planes] + pad_ref[f, (p + 1) % planes]
+            total = total + pltpu.roll(x, 1, 0) + pltpu.roll(x, 15, 0)
+            total = total + jnp.where(lane == 0, 0.0, pltpu.roll(x, 1, 1))
+            total = total + jnp.where(lane == rows - 1, 0.0, pltpu.roll(x, rows - 1, 1))
+            spreads.append(total - 6.0 * x)
+        mid_ref[0, p], mid_ref[1, p] = react(pad_ref[0, p], pad_ref[1, p], *spreads)
+
+
 def step_kernel(
-    u_ref, v_ref, next_ref, near_ref, far_ref,
-    un_ref, vn_ref, back_ref, send_ref, pad_ref, mid_ref, done_ref, turn_ref,
+    mid_ref, edge_ref, near_ref, far_ref,
+    un_ref, vn_ref, back_ref, send_ref, full_ref, done_ref, turn_ref,
 ):
-    right = lane_ids((16, 128)) % 4 < 2
-    beside = jnp.where(right != odd("gx"), near_ref[...], far_ref[...])
-    for f, ref in enumerate((u_ref, v_ref)):
-        pad_ref[f, :, 10:14, 0:rows] = jnp.zeros((planes, 4, rows), f32)
-        pad_ref[f, :, 0:6, 0:rows] = ref[:, 2:8, :]
-        pad_ref[f, :, 6:10, 0:rows] = next_ref[f]
-        pad_ref[f, :, 14:16, 0:rows] = ref[:, 0:2, :]
+    lane = lane_ids((16, 128))
+    edge = edge_ref[...]
+    beside = jnp.where((lane % 4 < 2) != odd("gx"), near_ref[...], far_ref[...])
+
+    place = (lane + 2) % 64
+    total = jnp.where(place < 4, pltpu.roll(beside, 68, 1), pltpu.roll(beside, 4, 1))
+    total = total + jnp.where(place >= 60, pltpu.roll(beside, 60, 1), pltpu.roll(beside, 124, 1))
+    total = total + pltpu.roll(beside, 1, 0) + pltpu.roll(beside, 15, 0)
+    total = total + jnp.where(
+        lane % 4 == 3,
+        pltpu.roll(beside, 1, 1) + pltpu.roll(edge, 127, 1),
+        pltpu.roll(edge, 1, 1) + pltpu.roll(beside, 127, 1),
+    )
+    spread = total - 6.0 * beside
+    other = pltpu.roll(beside, 64, 1)
+    first = (lane + 2) % 128 < 64
+    outer = react(jnp.where(first, beside, other), jnp.where(first, other, beside), spread, spread)
+    outer = jnp.where(first, *outer)
+
+    for f, rate in enumerate((substrate_diffusion, catalyst_diffusion)):
         for p in range(planes):
             q = f * planes + p
-            pad_ref[f, p, :, rows : rows + 128] = pltpu.roll(beside, (128 - 4 * q) % 128, 1)
-
+            left = jnp.where(lane == 0, pltpu.roll(beside, (1 - 4 * q) % 128, 1), 0.0)
+            right = jnp.where(lane == 127, pltpu.roll(beside, (127 - 4 * q) % 128, 1), 0.0)
+            full_ref[f, p, :, 0:128] = mid_ref[f, p, :, 0:128] + rate * left
+            full_ref[f, p, :, 128:256] = mid_ref[f, p, :, 128:256] + rate * right
+
+    outer = outer[0:8]
+    lane = lane_ids((8, rows))
     for p in range(planes):
-        below, above = (p - 1) % planes, (p + 1) % planes
-        u, v = pad_ref[0, p], pad_ref[1, p]
-        spread_u = neighbours(u, pad_ref[0, below], pad_ref[0, above])
-        spread_v = neighbours(v, pad_ref[1, below], pad_ref[1, above])
-        new_u, new_v = react(u, v, spread_u, spread_v)
-        mid_ref[0, p] = new_u
-        mid_ref[1, p] = new_v
-
-    for p in range(planes):
-        below, above = (p - 1) % planes, (p + 1) % planes
-        u, v = mid_ref[0, p], mid_ref[1, p]
-        spread_u = neighbours(u, mid_ref[0, below], mid_ref[0, above])
-        spread_v = neighbours(v, mid_ref[1, below], mid_ref[1, above])
-        new_u, new_v = react(u, v, spread_u, spread_v)
-        for f, (ref, new) in enumerate(((un_ref, new_u), (vn_ref, new_v))):
-            ref[p] = new[0:8, 0:rows]
-            back_ref[f, p] = new[6:8, 0:rows]
+        spreads = []
+        for f in range(2):
+            q = f * planes + p
+            x = full_ref[f, p]
+            total = full_ref[f, (p - 1) % planes, 0:8, :] + full_ref[f, (p + 1) % planes, 0:8, :]
+            total = total + pltpu.roll(x, 1, 0)[0:8] + pltpu.roll(x, 15, 0)[0:8]
+            x = x[0:8]
+            left = pltpu.roll(outer, (1 - 4 * q) % 128, 1)
+            right = pltpu.roll(outer, (127 - 4 * q) % 128, 1)
+            ends = jnp.concatenate([left, right], axis=1)
+            total = total + jnp.where(lane == 0, ends, pltpu.roll(x, 1, 1))
+            total = total + jnp.where(lane == rows - 1, ends, pltpu.roll(x, rows - 1, 1))
+            spreads.append(total - 6.0 * x)
+        news = react(full_ref[0, p, 0:8, :], full_ref[1, p, 0:8, :], *spreads)
+        for f, (ref, new) in enumerate(zip((un_ref, vn_ref), news)):
+            ref[p] = new
+            back_ref[f, p] = new[6:8]
             at = 8 * (f * planes + p)
             for t in range(2):
-                done_ref[t, at : at + 8, :] = new[0:8, 128 * t : 128 * t + 128]
+                done_ref[t, at : at + 8, :] = new[:, 128 * t : 128 * t + 128]
 
     many = 2 * planes
     for t in range(2):
@@ -196,11 +226,12 @@
     edge = call(edge_kernel, shape(16, 128), [(2 * planes, 2, 16, 128)])(u, v, after)
     far = lax.ppermute(edge, "gx", pairs("gx", 1))
     near = lax.ppermute(edge, "gx", pairs("gx", 0))
-    padded = (2, planes, 16, rows + 128)
+    padded = (2, planes, 16, rows)
+    mid = call(inner_kernel, pltpu.VMEM(padded, f32), [padded])(u, v, after, edge)
     un, vn, back, send = call(
         step_kernel, (inside, inside, shape(2, planes, 2, rows), shape(128, 128)),
-        [padded, padded, (2, 256, 128), (rows, 128)],
-    )(u, v, after, near, far)
+        [padded, (2, 256, 128), (rows, 128)],
+    )(mid, edge, near, far)
     back = lax.ppermute(back, "gy", ring("gy", 1))
     un, vn = call(join_kernel, (brick, brick))(un, vn, back)
     order = [(i + master) % owners for i in range(owners)]

time: 67.9 us -> 67.5 us (level)
  transfers between devices with their start and end apart: 5 -> 5, of which waited for: 4 -> 4; matrix products, arithmetic and copies ran while one was open for 0% -> 0% of each run, Pallas kernels for 1% -> 2%
where the time goes in v5:
time: 67.5 us; the launch traced here: 66.8 us
  starting transfers between devices  46.3 us (69%)
  waiting for transfers between devices  15 us (22%)
  Pallas kernels  4.68 us (7%)
  between operations  0.71 us (1%)
    all_to_all x1, starting transfers between devices, body(): lax.all_to_all(send.reshape(owners, 2, 128), 'gy', 0, 0, tiled=True, axis...  31.8 us
    ppermute x1, waiting for transfers between devices, body(): after = lax.ppermute(first, 'gy', ring('gy', -1))  6.38 us
    all_to_all x1, waiting for transfers between devices, body(): lax.all_to_all(send.reshape(owners, 2, 128), 'gy', 0, 0, tiled=True, axis...  6.38 us
    ppermute x1, starting transfers between devices, body(): back = lax.ppermute(back, 'gy', ring('gy', 1))  5.78 us
    ppermute x1, starting transfers between devices, body(): near = lax.ppermute(edge, 'gx', pairs('gx', 0))  3.68 us
    ppermute x1, starting transfers between devices, body(): after = lax.ppermute(first, 'gy', ring('gy', -1))  3.14 us
    ppermute x1, starting transfers between devices, body(): far = lax.ppermute(edge, 'gx', pairs('gx', 1))  1.91 us
    ppermute x1, waiting for transfers between devices, body(): back = lax.ppermute(back, 'gy', ring('gy', 1))  1.9 us
  transfers between devices with their start and end apart: 5, of which 4 were waited for; matrix products, arithmetic and copies ran while one was open for 0% of the time, Pallas kernels for 2%

profile of v5, /device:TPU:24, one launch (start us, length us, event | category | flops | bytes accessed | tf_op | source)
XLA Modules:
  0.0 66.8 jit_solution(15474188037293348560)
XLA Ops:
  0.6 0.0 copy-start.1
  0.6 0.0 copy-start
  0.6 0.9 %shard_map.49 = f32[2,16,4,256]{3,2,1,0:T(4,128)S(1)} custom-call(f32[16,8,256]{2,1,0:T(8,128)} %u_ref.3, f32[16,8,256]{2,1,0:T(8,128)} %v_ref.3), custom_call_target="tpu_custom_call" | custom-call | tf_op jit(solution)/shard_map/pallas_call | solution.py:221
  1.5 3.1 %collective-permute-start = (f32[2,16,4,256]{3,2,1,0:T(4,128)S(1)}, f32[2,16,4,256]{3,2,1,0:T(4,128)S(1)}, u32[]{:S(2)}, u32[]{:S(2)}) collective-permute-start(f32[2,16,4,256]{3,2,1,0:T(4,128)S(1)} %shard_map.49), channel_id=1, source_target_pairs={{0,63},{1,0},{2,1},{3,2},{4,3},{5,4},{6,5},{7,6},{8,7},{9,8},{10,9... | collective-permute-start | bytes 393224 | tf_op jit(solution)/shard_map/ppermute | solution.py:225
  4.7 6.4 %collective-permute-done.next_ref = f32[2,16,4,256]{3,2,1,0:T(4,128)S(1)} collective-permute-done((f32[2,16,4,256]{3,2,1,0:T(4,128)S(1)}, f32[2,16,4,256]{3,2,1,0:T(4,128)S(1)}, u32[]{:S(2)}, u32[]{:S(2)}) %collective-permute-start) | collective-permute-done | bytes 131104 | tf_op jit(solution)/shard_map/ppermute | solution.py:225
  11.1 0.0 copy-done.1
  11.1 0.0 copy-done
  11.1 0.2 shard_map.50.edge_ref
  11.3 1.9 %collective-permute-start.2 = (f32[16,128]{1,0:T(8,128)S(1)}, f32[16,128]{1,0:T(8,128)S(1)}, u32[]{:S(2)}, u32[]{:S(2)}) collective-permute-start(f32[16,128]{1,0:T(8,128)S(1)} %shard_map.50.edge_ref), channel_id=1, source_target_pairs={{64,128},{192,256},{320,384},{448,512},{576,640},{704,768},{832,89... | collective-permute-start | bytes 24584 | tf_op jit(solution)/shard_map/ppermute | solution.py:227
  13.2 3.7 %collective-permute-start.1 = (f32[16,128]{1,0:T(8,128)S(1)}, f32[16,128]{1,0:T(8,128)S(1)}, u32[]{:S(2)}, u32[]{:S(2)}) collective-permute-start(f32[16,128]{1,0:T(8,128)S(1)} %shard_map.50.edge_ref), channel_id=1, source_target_pairs={{0,64},{128,192},{256,320},{384,448},{512,576},{640,704},{768,832}... | collective-permute-start | bytes 24584 | tf_op jit(solution)/shard_map/ppermute | solution.py:228
  16.9 0.4 shard_map.51.mid_ref
  17.3 0.0 collective-permute-done.2.far_ref
  17.3 0.3 collective-permute-done.1.near_ref
  17.7 1.3 %shard_map.52 = (f32[16,8,256]{2,1,0:T(8,128)S(1)}, f32[16,8,256]{2,1,0:T(8,128)S(1)}, f32[2,16,2,256]{3,2,1,0:T(2,128)S(1)}, f32[128,128]{1,0:T(8,128)}) custom-call(f32[2,16,16,256]{3,2,1,0:T(8,128)S(1)} %shard_map.51.mid_ref, f32[16,128]{1,0:T(8,128)S(1)} %shard_map.50.edge_ref, f32[16,128]{1,0:T(8,128)S(1)} %collective-permute-done.1.near_ref, ...), custom_call_target="tpu_custom_call" | custom-call | tf_op jit(solution)/shard_map/pallas_call | solution.py:231
  18.9 31.8 %all-to-all-start = ((f32[64,2,128]{2,1,0:T(2,128)}), f32[64,2,128]{2,1,0:T(2,128)S(1)}, u32[]{:S(2)}, u32[]{:S(2)}) async-start(f32[64,2,128]{2,1,0:T(2,128)} %bitcast), calls=%async_computation | async-start | bytes 131072 | tf_op jit(solution)/shard_map/all_to_all | solution.py:238
  50.8 5.8 %collective-permute-start.3 = (f32[2,16,2,256]{3,2,1,0:T(2,128)S(1)}, f32[2,16,2,256]{3,2,1,0:T(2,128)S(1)}, u32[]{:S(2)}, u32[]{:S(2)}) collective-permute-start(f32[2,16,2,256]{3,2,1,0:T(2,128)S(1)} %get-tuple-element.11), channel_id=1, source_target_pairs={{0,1},{1,2},{2,3},{3,4},{4,5},{5,6},{6,7},{7,8},{8,9},{9,10},{10,1... | collective-permute-start | bytes 196616 | tf_op jit(solution)/shard_map/ppermute | solution.py:235
  56.6 1.9 %collective-permute-done.3.back_ref = f32[2,16,2,256]{3,2,1,0:T(2,128)S(1)} collective-permute-done((f32[2,16,2,256]{3,2,1,0:T(2,128)S(1)}, f32[2,16,2,256]{3,2,1,0:T(2,128)S(1)}, u32[]{:S(2)}, u32[]{:S(2)}) %collective-permute-start.3) | collective-permute-done | bytes 65568 | tf_op jit(solution)/shard_map/ppermute | solution.py:235
  58.5 0.8 %shard_map.53 = (f32[16,8,256]{2,1,0:T(8,128)}, f32[16,8,256]{2,1,0:T(8,128)}) custom-call(f32[16,8,256]{2,1,0:T(8,128)S(1)} %get-tuple-element.9.un_ref, f32[16,8,256]{2,1,0:T(8,128)S(1)} %get-tuple-element.10.vn_ref, f32[2,16,2,256]{3,2,1,0:T(2,128)S(1)} %collective-permute-done.3.back_ref), custom_call_target="tpu_custom_call" | custom-call | tf_op jit(solution)/shard_map/pallas_call | solution.py:236
  59.2 6.4 %all-to-all-done = f32[64,2,128]{2,1,0:T(2,128)S(1)} async-done(((f32[64,2,128]{2,1,0:T(2,128)}), f32[64,2,128]{2,1,0:T(2,128)S(1)}, u32[]{:S(2)}, u32[]{:S(2)}) %all-to-all-start) | async-done | bytes 65568 | tf_op jit(solution)/shard_map/all_to_all | solution.py:238
  65.6 1.2 %shard_map.54 = f32[512,128]{1,0:T(8,128)} custom-call(f32[128,128]{1,0:T(8,128)S(1)} %bitcast.7), custom_call_target="tpu_custom_call" | custom-call | tf_op jit(solution)/shard_map/pallas_call | solution.py:241
Async XLA Ops:
  0.6 10.4 %copy-start.1 = (f32[16,8,256]{2,1,0:T(8,128)S(1)}, f32[16,8,256]{2,1,0:T(8,128)}, u32[]{:S(2)}) copy-start(f32[16,8,256]{2,1,0:T(8,128)} %v_ref.3) | copy-start | bytes 393220
  0.6 10.4 %copy-start = (f32[16,8,256]{2,1,0:T(8,128)S(1)}, f32[16,8,256]{2,1,0:T(8,128)}, u32[]{:S(2)}) copy-start(f32[16,8,256]{2,1,0:T(8,128)} %u_ref.3) | copy-start | bytes 393220
  1.5 9.5 %collective-permute-start = (f32[2,16,4,256]{3,2,1,0:T(4,128)S(1)}, f32[2,16,4,256]{3,2,1,0:T(4,128)S(1)}, u32[]{:S(2)}, u32[]{:S(2)}) collective-permute-start(f32[2,16,4,256]{3,2,1,0:T(4,128)S(1)} %shard_map.49), channel_id=1, source_target_pairs={{0,63},{1,0},{2,1},{3,2},{4,3},{5,4},{6,5},{7,6},{8,7},{9,8},{10,9... | collective-permute-start | bytes 393224 | tf_op jit(solution)/shard_map/ppermute | solution.py:225
  11.3 6.1 %collective-permute-start.2 = (f32[16,128]{1,0:T(8,128)S(1)}, f32[16,128]{1,0:T(8,128)S(1)}, u32[]{:S(2)}, u32[]{:S(2)}) collective-permute-start(f32[16,128]{1,0:T(8,128)S(1)} %shard_map.50.edge_ref), channel_id=1, source_target_pairs={{64,128},{192,256},{320,384},{448,512},{576,640},{704,768},{832,89... | collective-permute-start | bytes 24584 | tf_op jit(solution)/shard_map/ppermute | solution.py:227
  13.2 4.5 %collective-permute-start.1 = (f32[16,128]{1,0:T(8,128)S(1)}, f32[16,128]{1,0:T(8,128)S(1)}, u32[]{:S(2)}, u32[]{:S(2)}) collective-permute-start(f32[16,128]{1,0:T(8,128)S(1)} %shard_map.50.edge_ref), channel_id=1, source_target_pairs={{0,64},{128,192},{256,320},{384,448},{512,576},{640,704},{768,832}... | collective-permute-start | bytes 24584 | tf_op jit(solution)/shard_map/ppermute | solution.py:228
  18.9 46.6 %all-to-all-start = ((f32[64,2,128]{2,1,0:T(2,128)}), f32[64,2,128]{2,1,0:T(2,128)S(1)}, u32[]{:S(2)}, u32[]{:S(2)}) async-start(f32[64,2,128]{2,1,0:T(2,128)} %bitcast), calls=%async_computation | async-start | bytes 131072 | tf_op jit(solution)/shard_map/all_to_all | solution.py:238
  50.8 7.7 %collective-permute-start.3 = (f32[2,16,2,256]{3,2,1,0:T(2,128)S(1)}, f32[2,16,2,256]{3,2,1,0:T(2,128)S(1)}, u32[]{:S(2)}, u32[]{:S(2)}) collective-permute-start(f32[2,16,2,256]{3,2,1,0:T(2,128)S(1)} %get-tuple-element.11), channel_id=1, source_target_pairs={{0,1},{1,2},{2,3},{3,4},{4,5},{5,6},{6,7},{7,8},{8,9},{9,10},{10,1... | collective-permute-start | bytes 196616 | tf_op jit(solution)/shard_map/ppermute | solution.py:235

commit v6 on v5

--- a/solution.py
+++ b/solution.py
@@ -38,6 +38,18 @@
         copy.wait()
         at = slice(h * part, h * part + part)
         first_ref[f, at] = (u_ref, v_ref)[f][at, 0:4, :]
+
+
+def fetch_kernel(u_hbm, v_hbm, first_ref, u_ref, v_ref, sems):
+    del first_ref
+    copies = [
+        pltpu.make_async_copy(src, dst, sems.at[f])
+        for f, (src, dst) in enumerate(((u_hbm, u_ref), (v_hbm, v_ref)))
+    ]
+    for copy in copies:
+        copy.start()
+    for copy in copies:
+        copy.wait()
 
 
 def edge_kernel(u_ref, v_ref, next_ref, edge_ref, pad_ref):
@@ -110,15 +122,20 @@
     outer = react(jnp.where(first, beside, other), jnp.where(first, other, beside), spread, spread)
     outer = jnp.where(first, *outer)
 
+    def swap(x):
+        return jnp.where(lane_ids(x.shape) % 4 == 0, pltpu.roll(x, 1, 1), pltpu.roll(x, 127, 1))
+
+    beside = swap(beside)
     for f, rate in enumerate((substrate_diffusion, catalyst_diffusion)):
         for p in range(planes):
             q = f * planes + p
-            left = jnp.where(lane == 0, pltpu.roll(beside, (1 - 4 * q) % 128, 1), 0.0)
-            right = jnp.where(lane == 127, pltpu.roll(beside, (127 - 4 * q) % 128, 1), 0.0)
+            ends = pltpu.roll(beside, -4 * q % 128, 1)
+            left = jnp.where(lane == 0, ends, 0.0)
+            right = jnp.where(lane == 127, ends, 0.0)
             full_ref[f, p, :, 0:128] = mid_ref[f, p, :, 0:128] + rate * left
             full_ref[f, p, :, 128:256] = mid_ref[f, p, :, 128:256] + rate * right
 
-    outer = outer[0:8]
+    outer = swap(outer[0:8])
     lane = lane_ids((8, rows))
     for p in range(planes):
         spreads = []
@@ -128,9 +145,8 @@
             total = full_ref[f, (p - 1) % planes, 0:8, :] + full_ref[f, (p + 1) % planes, 0:8, :]
             total = total + pltpu.roll(x, 1, 0)[0:8] + pltpu.roll(x, 15, 0)[0:8]
             x = x[0:8]
-            left = pltpu.roll(outer, (1 - 4 * q) % 128, 1)
-            right = pltpu.roll(outer, (127 - 4 * q) % 128, 1)
-            ends = jnp.concatenate([left, right], axis=1)
+            ends = pltpu.roll(outer, -4 * q % 128, 1)
+            ends = jnp.concatenate([ends, ends], axis=1)
             total = total + jnp.where(lane == 0, ends, pltpu.roll(x, 1, 1))
             total = total + jnp.where(lane == rows - 1, ends, pltpu.roll(x, rows - 1, 1))
             spreads.append(total - 6.0 * x)
@@ -223,6 +239,10 @@
         limit=large, in_specs=[pl.BlockSpec(memory_space=pltpu.HBM)] * 2,
     )(u, v)
     after = lax.ppermute(first, "gy", ring("gy", -1))
+    u, v = call(
+        fetch_kernel, (inside, inside), sems=[(2,)], limit=large,
+        in_specs=[pl.BlockSpec(memory_space=pltpu.HBM)] * 2 + [pl.BlockSpec(memory_space=pltpu.VMEM)],
+    )(u, v, first)
     edge = call(edge_kernel, shape(16, 128), [(2 * planes, 2, 16, 128)])(u, v, after)
     far = lax.ppermute(edge, "gx", pairs("gx", 1))
     near = lax.ppermute(edge, "gx", pairs("gx", 0))

time: 67.5 us -> 67.5 us (level)
  waiting for transfers between devices: 15 us -> 13.1 us
  Pallas kernels: 4.68 us -> 6.53 us
    ppermute x1, waiting for transfers between devices: 6.38 us -> 4.47 us  [body(): after = lax.ppermute(first, 'gy', ring('gy', -1))]
    pallas_call x0 -> x1, Pallas kernels: none -> 1.89 us  [body(): call(fetch_kernel, (inside, inside), sems=[(2,)], limit=large, in_specs=[...]
  transfers between devices with their start and end apart: 5 -> 5, of which waited for: 4 -> 4; matrix products, arithmetic and copies ran while one was open for 0% -> 0% of each run, Pallas kernels for 2% -> 5%
where the time goes in v6:
time: 67.5 us; the launch traced here: 66.7 us
  starting transfers between devices  46.3 us (69%)
  waiting for transfers between devices  13.1 us (19%)
  Pallas kernels  6.53 us (10%)
  between operations  0.72 us (1%)
    all_to_all x1, starting transfers between devices, body(): lax.all_to_all(send.reshape(owners, 2, 128), 'gy', 0, 0, tiled=True, axis...  31.8 us
    all_to_all x1, waiting for transfers between devices, body(): lax.all_to_all(send.reshape(owners, 2, 128), 'gy', 0, 0, tiled=True, axis...  6.38 us
    ppermute x1, starting transfers between devices, body(): back = lax.ppermute(back, 'gy', ring('gy', 1))  5.78 us
    ppermute x1, waiting for transfers between devices, body(): after = lax.ppermute(first, 'gy', ring('gy', -1))  4.47 us
    ppermute x1, starting transfers between devices, body(): near = lax.ppermute(edge, 'gx', pairs('gx', 0))  3.68 us
    ppermute x1, starting transfers between devices, body(): after = lax.ppermute(first, 'gy', ring('gy', -1))  3.14 us
    ppermute x1, starting transfers between devices, body(): far = lax.ppermute(edge, 'gx', pairs('gx', 1))  1.91 us
    ppermute x1, waiting for transfers between devices, body(): back = lax.ppermute(back, 'gy', ring('gy', 1))  1.9 us
  transfers between devices with their start and end apart: 5, of which 4 were waited for; matrix products, arithmetic and copies ran while one was open for 0% of the time, Pallas kernels for 5%

profile of v6, /device:TPU:24, one launch (start us, length us, event | category | flops | bytes accessed | tf_op | source)
XLA Modules:
  0.0 66.7 jit_solution(17157598543893706993)
XLA Ops:
  0.6 0.8 %shard_map.49.first_ref = f32[2,16,4,256]{3,2,1,0:T(4,128)S(1)} custom-call(f32[16,8,256]{2,1,0:T(8,128)} %u_hbm.3, f32[16,8,256]{2,1,0:T(8,128)} %v_hbm.3), custom_call_target="tpu_custom_call" | custom-call | tf_op jit(solution)/shard_map/pallas_call | solution.py:237
  1.5 0.0 copy-start
  1.5 3.1 %collective-permute-start = (f32[2,16,4,256]{3,2,1,0:T(4,128)S(1)}, f32[2,16,4,256]{3,2,1,0:T(4,128)S(1)}, u32[]{:S(2)}, u32[]{:S(2)}) collective-permute-start(f32[2,16,4,256]{3,2,1,0:T(4,128)S(1)} %shard_map.49.first_ref), channel_id=1, source_target_pairs={{0,63},{1,0},{2,1},{3,2},{4,3},{5,4},{6,5},{7,6},{8,7},{9,8},{10,9... | collective-permute-start | bytes 393224 | tf_op jit(solution)/shard_map/ppermute | solution.py:241
  4.6 0.0 copy-done
  4.7 1.9 %shard_map.50 = (f32[16,8,256]{2,1,0:T(8,128)S(1)}, f32[16,8,256]{2,1,0:T(8,128)S(1)}) custom-call(f32[16,8,256]{2,1,0:T(8,128)} %u_hbm.3, f32[16,8,256]{2,1,0:T(8,128)} %v_hbm.3, f32[2,16,4,256]{3,2,1,0:T(4,128)} %copy-done), custom_call_target="tpu_custom_call" | custom-call | tf_op jit(solution)/shard_map/pallas_call | solution.py:242
  6.6 4.5 %collective-permute-done.next_ref = f32[2,16,4,256]{3,2,1,0:T(4,128)S(1)} collective-permute-done((f32[2,16,4,256]{3,2,1,0:T(4,128)S(1)}, f32[2,16,4,256]{3,2,1,0:T(4,128)S(1)}, u32[]{:S(2)}, u32[]{:S(2)}) %collective-permute-start) | collective-permute-done | bytes 131104 | tf_op jit(solution)/shard_map/ppermute | solution.py:241
  11.0 0.2 shard_map.51.edge_ref
  11.2 1.9 %collective-permute-start.2 = (f32[16,128]{1,0:T(8,128)S(1)}, f32[16,128]{1,0:T(8,128)S(1)}, u32[]{:S(2)}, u32[]{:S(2)}) collective-permute-start(f32[16,128]{1,0:T(8,128)S(1)} %shard_map.51.edge_ref), channel_id=1, source_target_pairs={{64,128},{192,256},{320,384},{448,512},{576,640},{704,768},{832,89... | collective-permute-start | bytes 24584 | tf_op jit(solution)/shard_map/ppermute | solution.py:247
  13.1 3.7 %collective-permute-start.1 = (f32[16,128]{1,0:T(8,128)S(1)}, f32[16,128]{1,0:T(8,128)S(1)}, u32[]{:S(2)}, u32[]{:S(2)}) collective-permute-start(f32[16,128]{1,0:T(8,128)S(1)} %shard_map.51.edge_ref), channel_id=1, source_target_pairs={{0,64},{128,192},{256,320},{384,448},{512,576},{640,704},{768,832}... | collective-permute-start | bytes 24584 | tf_op jit(solution)/shard_map/ppermute | solution.py:248
  16.8 0.4 shard_map.52.mid_ref
  17.3 0.0 collective-permute-done.2.far_ref
  17.3 0.3 collective-permute-done.1.near_ref
  17.6 1.3 %shard_map.53 = (f32[16,8,256]{2,1,0:T(8,128)S(1)}, f32[16,8,256]{2,1,0:T(8,128)S(1)}, f32[2,16,2,256]{3,2,1,0:T(2,128)S(1)}, f32[128,128]{1,0:T(8,128)}) custom-call(f32[2,16,16,256]{3,2,1,0:T(8,128)S(1)} %shard_map.52.mid_ref, f32[16,128]{1,0:T(8,128)S(1)} %shard_map.51.edge_ref, f32[16,128]{1,0:T(8,128)S(1)} %collective-permute-done.1.near_ref, ...), custom_call_target="tpu_custom_call" | custom-call | tf_op jit(solution)/shard_map/pallas_call | solution.py:251
  18.9 31.8 %all-to-all-start = ((f32[64,2,128]{2,1,0:T(2,128)}), f32[64,2,128]{2,1,0:T(2,128)S(1)}, u32[]{:S(2)}, u32[]{:S(2)}) async-start(f32[64,2,128]{2,1,0:T(2,128)} %bitcast), calls=%async_computation | async-start | bytes 131072 | tf_op jit(solution)/shard_map/all_to_all | solution.py:258
  50.7 5.8 %collective-permute-start.3 = (f32[2,16,2,256]{3,2,1,0:T(2,128)S(1)}, f32[2,16,2,256]{3,2,1,0:T(2,128)S(1)}, u32[]{:S(2)}, u32[]{:S(2)}) collective-permute-start(f32[2,16,2,256]{3,2,1,0:T(2,128)S(1)} %get-tuple-element.15), channel_id=1, source_target_pairs={{0,1},{1,2},{2,3},{3,4},{4,5},{5,6},{6,7},{7,8},{8,9},{9,10},{10,1... | collective-permute-start | bytes 196616 | tf_op jit(solution)/shard_map/ppermute | solution.py:255
  56.5 1.9 %collective-permute-done.3.back_ref = f32[2,16,2,256]{3,2,1,0:T(2,128)S(1)} collective-permute-done((f32[2,16,2,256]{3,2,1,0:T(2,128)S(1)}, f32[2,16,2,256]{3,2,1,0:T(2,128)S(1)}, u32[]{:S(2)}, u32[]{:S(2)}) %collective-permute-start.3) | collective-permute-done | bytes 65568 | tf_op jit(solution)/shard_map/ppermute | solution.py:255
  58.4 0.8 %shard_map.54 = (f32[16,8,256]{2,1,0:T(8,128)}, f32[16,8,256]{2,1,0:T(8,128)}) custom-call(f32[16,8,256]{2,1,0:T(8,128)S(1)} %get-tuple-element.13.un_ref, f32[16,8,256]{2,1,0:T(8,128)S(1)} %get-tuple-element.14.vn_ref, f32[2,16,2,256]{3,2,1,0:T(2,128)S(1)} %collective-permute-done.3.back_ref), custom_call_target="tpu_custom_call" | custom-call | tf_op jit(solution)/shard_map/pallas_call | solution.py:256
  59.2 6.4 %all-to-all-done = f32[64,2,128]{2,1,0:T(2,128)S(1)} async-done(((f32[64,2,128]{2,1,0:T(2,128)}), f32[64,2,128]{2,1,0:T(2,128)S(1)}, u32[]{:S(2)}, u32[]{:S(2)}) %all-to-all-start) | async-done | bytes 65568 | tf_op jit(solution)/shard_map/all_to_all | solution.py:258
  65.5 1.2 %shard_map.55 = f32[512,128]{1,0:T(8,128)} custom-call(f32[128,128]{1,0:T(8,128)S(1)} %bitcast.7), custom_call_target="tpu_custom_call" | custom-call | tf_op jit(solution)/shard_map/pallas_call | solution.py:261
Async XLA Ops:
  1.5 3.2 %copy-start = (f32[2,16,4,256]{3,2,1,0:T(4,128)}, f32[2,16,4,256]{3,2,1,0:T(4,128)S(1)}, u32[]{:S(2)}) copy-start(f32[2,16,4,256]{3,2,1,0:T(4,128)S(1)} %shard_map.49.first_ref) | copy-start | bytes 393220
  1.5 9.5 %collective-permute-start = (f32[2,16,4,256]{3,2,1,0:T(4,128)S(1)}, f32[2,16,4,256]{3,2,1,0:T(4,128)S(1)}, u32[]{:S(2)}, u32[]{:S(2)}) collective-permute-start(f32[2,16,4,256]{3,2,1,0:T(4,128)S(1)} %shard_map.49.first_ref), channel_id=1, source_target_pairs={{0,63},{1,0},{2,1},{3,2},{4,3},{5,4},{6,5},{7,6},{8,7},{9,8},{10,9... | collective-permute-start | bytes 393224 | tf_op jit(solution)/shard_map/ppermute | solution.py:241
  11.2 6.1 %collective-permute-start.2 = (f32[16,128]{1,0:T(8,128)S(1)}, f32[16,128]{1,0:T(8,128)S(1)}, u32[]{:S(2)}, u32[]{:S(2)}) collective-permute-start(f32[16,128]{1,0:T(8,128)S(1)} %shard_map.51.edge_ref), channel_id=1, source_target_pairs={{64,128},{192,256},{320,384},{448,512},{576,640},{704,768},{832,89... | collective-permute-start | bytes 24584 | tf_op jit(solution)/shard_map/ppermute | solution.py:247
  13.1 4.5 %collective-permute-start.1 = (f32[16,128]{1,0:T(8,128)S(1)}, f32[16,128]{1,0:T(8,128)S(1)}, u32[]{:S(2)}, u32[]{:S(2)}) collective-permute-start(f32[16,128]{1,0:T(8,128)S(1)} %shard_map.51.edge_ref), channel_id=1, source_target_pairs={{0,64},{128,192},{256,320},{384,448},{512,576},{640,704},{768,832}... | collective-permute-start | bytes 24584 | tf_op jit(solution)/shard_map/ppermute | solution.py:248
  18.9 46.6 %all-to-all-start = ((f32[64,2,128]{2,1,0:T(2,128)}), f32[64,2,128]{2,1,0:T(2,128)S(1)}, u32[]{:S(2)}, u32[]{:S(2)}) async-start(f32[64,2,128]{2,1,0:T(2,128)} %bitcast), calls=%async_computation | async-start | bytes 131072 | tf_op jit(solution)/shard_map/all_to_all | solution.py:258
  50.7 7.7 %collective-permute-start.3 = (f32[2,16,2,256]{3,2,1,0:T(2,128)S(1)}, f32[2,16,2,256]{3,2,1,0:T(2,128)S(1)}, u32[]{:S(2)}, u32[]{:S(2)}) collective-permute-start(f32[2,16,2,256]{3,2,1,0:T(2,128)S(1)} %get-tuple-element.15), channel_id=1, source_target_pairs={{0,1},{1,2},{2,3},{3,4},{4,5},{5,6},{6,7},{7,8},{8,9},{9,10},{10,1... | collective-permute-start | bytes 196616 | tf_op jit(solution)/shard_map/ppermute | solution.py:255

commit v7 on v6

--- a/solution.py
+++ b/solution.py
@@ -13,7 +13,7 @@
 planes, cols, rows = 16, 8, 256
 owners = 64
 large = 56 * 1024 * 1024
-master = 43
+master = 45
 f32 = jnp.float32
 
 
@@ -187,7 +187,7 @@
         out[:, 2:8, :] = ref[:, 0:6, :]
 
 
-def rebuild_kernel(got_ref, out_ref, wide_ref):
+def rebuild_kernel(got_ref, out_hbm, wide_ref, out_ref, sems):
     got = pltpu.roll(got_ref[...], 2 * master, 0)
     even = lane_ids((128, 128)) % 64 < 32
     level1 = jnp.where(even, pltpu.roll(pltpu.roll(got, 1, 0), 96, 1), pltpu.roll(got, 32, 1))
@@ -198,12 +198,21 @@
     for d in range(2):
         wide_ref[pl.ds(d, 128, stride=4), :] = blend
         wide_ref[pl.ds(2 + d, 128, stride=4), :] = shifted
-    for t in range(4):
-        turned = wide_ref[128 * t : 128 * t + 128, :].T
-        for r in range(2):
-            part = turned[64 * r : 64 * r + 32]
-            for d in range(2):
-                out_ref[pl.ds(4 * t + 2 * r + d, 32, stride=16), :] = part
+    copies = []
+    for half in range(2):
+        for t in range(2):
+            at = 128 * (2 * half + t)
+            turned = wide_ref[at : at + 128, :].T
+            for r in range(2):
+                part = turned[64 * r : 64 * r + 32]
+                for d in range(2):
+                    out_ref[half, pl.ds(4 * t + 2 * r + d, 32, stride=8), :] = part
+        copies.append(pltpu.make_async_copy(
+            out_ref.at[half].reshape(32, 8, 128), out_hbm.at[:, pl.ds(8 * half, 8), :], sems.at[half]
+        ))
+        copies[-1].start()
+    for copy in copies:
+        copy.wait()
 
 
 def call(kernel, out_shape, scratch=(), sems=(), limit=32 * 1024 * 1024, **kw):
@@ -241,7 +250,7 @@
     after = lax.ppermute(first, "gy", ring("gy", -1))
     u, v = call(
         fetch_kernel, (inside, inside), sems=[(2,)], limit=large,
-        in_specs=[pl.BlockSpec(memory_space=pltpu.HBM)] * 2 + [pl.BlockSpec(memory_space=pltpu.VMEM)],
+        in_specs=[pl.BlockSpec(memory_space=pltpu.HBM)] * 2 + [pl.BlockSpec(memory_space=pl.ANY)],
     )(u, v, first)
     edge = call(edge_kernel, shape(16, 128), [(2 * planes, 2, 16, 128)])(u, v, after)
     far = lax.ppermute(edge, "gx", pairs("gx", 1))
@@ -258,7 +267,10 @@
     got = lax.all_to_all(
         send.reshape(owners, 2, 128), "gy", 0, 0, tiled=True, axis_index_groups=[order]
     )
-    out = call(rebuild_kernel, shape(512, 128), [(512, 128)])(got.reshape(128, 128))
+    out = call(
+        rebuild_kernel, shape(32, 16, 128), [(512, 128), (2, 256, 128)], [(2,)],
+        out_specs=pl.BlockSpec(memory_space=pl.ANY),
+    )(got.reshape(128, 128))
     out = out.reshape(2, planes, 4, 4, 128).transpose(0, 1, 3, 2, 4).reshape(2, planes, 4, 512)
     return un, vn, out
 

time: 67.5 us -> 67.5 us (level)
  waiting for transfers between devices: 13.1 us -> 14.9 us
  Pallas kernels: 6.53 us -> 5.6 us
  starting transfers between devices: 46.3 us -> 45.4 us
    all_to_all x1, waiting for transfers between devices: 6.38 us -> 7.32 us  [body(): lax.all_to_all(send.reshape(owners, 2, 128), 'gy', 0, 0, tiled=True, axis...]
    all_to_all x1, starting transfers between devices: 31.8 us -> 30.9 us  [body(): lax.all_to_all(send.reshape(owners, 2, 128), 'gy', 0, 0, tiled=True, axis...]
    pallas_call x1, Pallas kernels: 1.89 us -> 0.99 us  [body(): call(fetch_kernel, (inside, inside), sems=[(2,)], limit=large, in_specs=[...]
    ppermute x1, waiting for transfers between devices: 4.47 us -> 5.38 us  [body(): after = lax.ppermute(first, 'gy', ring('gy', -1))]
  transfers between devices with their start and end apart: 5 -> 5, of which waited for: 4 -> 4; matrix products, arithmetic and copies ran while one was open for 0% -> 0% of each run, Pallas kernels for 5% -> 3%
where the time goes in v7:
time: 67.5 us; the launch traced here: 66.7 us
  starting transfers between devices  45.4 us (67%)
  waiting for transfers between devices  14.9 us (22%)
  Pallas kernels  5.6 us (8%)
  between operations  0.72 us (1%)
    all_to_all x1, starting transfers between devices, body(): lax.all_to_all(send.reshape(owners, 2, 128), 'gy', 0, 0, tiled=True, axis...  30.9 us
    all_to_all x1, waiting for transfers between devices, body(): lax.all_to_all(send.reshape(owners, 2, 128), 'gy', 0, 0, tiled=True, axis...  7.32 us
    ppermute x1, starting transfers between devices, body(): back = lax.ppermute(back, 'gy', ring('gy', 1))  5.78 us
    ppermute x1, waiting for transfers between devices, body(): after = lax.ppermute(first, 'gy', ring('gy', -1))  5.38 us
    ppermute x1, starting transfers between devices, body(): near = lax.ppermute(edge, 'gx', pairs('gx', 0))  3.68 us
    ppermute x1, starting transfers between devices, body(): after = lax.ppermute(first, 'gy', ring('gy', -1))  3.14 us
    ppermute x1, starting transfers between devices, body(): far = lax.ppermute(edge, 'gx', pairs('gx', 1))  1.91 us
    ppermute x1, waiting for transfers between devices, body(): back = lax.ppermute(back, 'gy', ring('gy', 1))  1.9 us
  transfers between devices with their start and end apart: 5, of which 4 were waited for; matrix products, arithmetic and copies ran while one was open for 0% of the time, Pallas kernels for 3%

profile of v7, /device:TPU:24, one launch (start us, length us, event | category | flops | bytes accessed | tf_op | source)
XLA Modules:
  0.0 66.7 jit_solution(147370376848131557)
XLA Ops:
  0.6 0.8 %shard_map.49.first_ref = f32[2,16,4,256]{3,2,1,0:T(4,128)S(1)} custom-call(f32[16,8,256]{2,1,0:T(8,128)} %u_hbm.3, f32[16,8,256]{2,1,0:T(8,128)} %v_hbm.3), custom_call_target="tpu_custom_call" | custom-call | tf_op jit(solution)/shard_map/pallas_call | solution.py:246
  1.5 0.0 copy-start
  1.5 3.1 %collective-permute-start = (f32[2,16,4,256]{3,2,1,0:T(4,128)S(1)}, f32[2,16,4,256]{3,2,1,0:T(4,128)S(1)}, u32[]{:S(2)}, u32[]{:S(2)}) collective-permute-start(f32[2,16,4,256]{3,2,1,0:T(4,128)S(1)} %shard_map.49.first_ref), channel_id=1, source_target_pairs={{0,63},{1,0},{2,1},{3,2},{4,3},{5,4},{6,5},{7,6},{8,7},{9,8},{10,9... | collective-permute-start | bytes 393224 | tf_op jit(solution)/shard_map/ppermute | solution.py:250
  4.6 0.0 copy-done
  4.7 1.0 %shard_map.50 = (f32[16,8,256]{2,1,0:T(8,128)S(1)}, f32[16,8,256]{2,1,0:T(8,128)S(1)}) custom-call(f32[16,8,256]{2,1,0:T(8,128)} %u_hbm.3, f32[16,8,256]{2,1,0:T(8,128)} %v_hbm.3, f32[2,16,4,256]{3,2,1,0:T(4,128)} %copy-done), custom_call_target="tpu_custom_call" | custom-call | tf_op jit(solution)/shard_map/pallas_call | solution.py:251
  5.7 5.4 %collective-permute-done.next_ref = f32[2,16,4,256]{3,2,1,0:T(4,128)S(1)} collective-permute-done((f32[2,16,4,256]{3,2,1,0:T(4,128)S(1)}, f32[2,16,4,256]{3,2,1,0:T(4,128)S(1)}, u32[]{:S(2)}, u32[]{:S(2)}) %collective-permute-start) | collective-permute-done | bytes 131104 | tf_op jit(solution)/shard_map/ppermute | solution.py:250
  11.0 0.2 shard_map.51.edge_ref
  11.2 1.9 %collective-permute-start.2 = (f32[16,128]{1,0:T(8,128)S(1)}, f32[16,128]{1,0:T(8,128)S(1)}, u32[]{:S(2)}, u32[]{:S(2)}) collective-permute-start(f32[16,128]{1,0:T(8,128)S(1)} %shard_map.51.edge_ref), channel_id=1, source_target_pairs={{64,128},{192,256},{320,384},{448,512},{576,640},{704,768},{832,89... | collective-permute-start | bytes 24584 | tf_op jit(solution)/shard_map/ppermute | solution.py:256
  13.1 3.7 %collective-permute-start.1 = (f32[16,128]{1,0:T(8,128)S(1)}, f32[16,128]{1,0:T(8,128)S(1)}, u32[]{:S(2)}, u32[]{:S(2)}) collective-permute-start(f32[16,128]{1,0:T(8,128)S(1)} %shard_map.51.edge_ref), channel_id=1, source_target_pairs={{0,64},{128,192},{256,320},{384,448},{512,576},{640,704},{768,832}... | collective-permute-start | bytes 24584 | tf_op jit(solution)/shard_map/ppermute | solution.py:257
  16.8 0.4 shard_map.52.mid_ref
  17.3 0.0 collective-permute-done.2.far_ref
  17.3 0.3 collective-permute-done.1.near_ref
  17.6 1.3 %shard_map.53 = (f32[16,8,256]{2,1,0:T(8,128)S(1)}, f32[16,8,256]{2,1,0:T(8,128)S(1)}, f32[2,16,2,256]{3,2,1,0:T(2,128)S(1)}, f32[128,128]{1,0:T(8,128)}) custom-call(f32[2,16,16,256]{3,2,1,0:T(8,128)S(1)} %shard_map.52.mid_ref, f32[16,128]{1,0:T(8,128)S(1)} %shard_map.51.edge_ref, f32[16,128]{1,0:T(8,128)S(1)} %collective-permute-done.1.near_ref, ...), custom_call_target="tpu_custom_call" | custom-call | tf_op jit(solution)/shard_map/pallas_call | solution.py:260
  18.9 30.9 %all-to-all-start = ((f32[64,2,128]{2,1,0:T(2,128)}), f32[64,2,128]{2,1,0:T(2,128)S(1)}, u32[]{:S(2)}, u32[]{:S(2)}) async-start(f32[64,2,128]{2,1,0:T(2,128)} %bitcast), calls=%async_computation | async-start | bytes 131072 | tf_op jit(solution)/shard_map/all_to_all | solution.py:267
  49.8 5.8 %collective-permute-start.3 = (f32[2,16,2,256]{3,2,1,0:T(2,128)S(1)}, f32[2,16,2,256]{3,2,1,0:T(2,128)S(1)}, u32[]{:S(2)}, u32[]{:S(2)}) collective-permute-start(f32[2,16,2,256]{3,2,1,0:T(2,128)S(1)} %get-tuple-element.15), channel_id=1, source_target_pairs={{0,1},{1,2},{2,3},{3,4},{4,5},{5,6},{6,7},{7,8},{8,9},{9,10},{10,1... | collective-permute-start | bytes 196616 | tf_op jit(solution)/shard_map/ppermute | solution.py:264
  55.6 1.9 %collective-permute-done.3.back_ref = f32[2,16,2,256]{3,2,1,0:T(2,128)S(1)} collective-permute-done((f32[2,16,2,256]{3,2,1,0:T(2,128)S(1)}, f32[2,16,2,256]{3,2,1,0:T(2,128)S(1)}, u32[]{:S(2)}, u32[]{:S(2)}) %collective-permute-start.3) | collective-permute-done | bytes 65568 | tf_op jit(solution)/shard_map/ppermute | solution.py:264
  57.5 0.8 %shard_map.54 = (f32[16,8,256]{2,1,0:T(8,128)}, f32[16,8,256]{2,1,0:T(8,128)}) custom-call(f32[16,8,256]{2,1,0:T(8,128)S(1)} %get-tuple-element.13.un_ref, f32[16,8,256]{2,1,0:T(8,128)S(1)} %get-tuple-element.14.vn_ref, f32[2,16,2,256]{3,2,1,0:T(2,128)S(1)} %collective-permute-done.3.back_ref), custom_call_target="tpu_custom_call" | custom-call | tf_op jit(solution)/shard_map/pallas_call | solution.py:265
  58.2 7.3 %all-to-all-done = f32[64,2,128]{2,1,0:T(2,128)S(1)} async-done(((f32[64,2,128]{2,1,0:T(2,128)}), f32[64,2,128]{2,1,0:T(2,128)S(1)}, u32[]{:S(2)}, u32[]{:S(2)}) %all-to-all-start) | async-done | bytes 65568 | tf_op jit(solution)/shard_map/all_to_all | solution.py:267
  65.6 1.1 %shard_map.55 = f32[32,16,128]{2,1,0:T(8,128)} custom-call(f32[128,128]{1,0:T(8,128)S(1)} %bitcast.7), custom_call_target="tpu_custom_call" | custom-call | tf_op jit(solution)/shard_map/pallas_call | solution.py:270
Async XLA Ops:
  1.5 3.2 %copy-start = (f32[2,16,4,256]{3,2,1,0:T(4,128)}, f32[2,16,4,256]{3,2,1,0:T(4,128)S(1)}, u32[]{:S(2)}) copy-start(f32[2,16,4,256]{3,2,1,0:T(4,128)S(1)} %shard_map.49.first_ref) | copy-start | bytes 393220
  1.5 9.5 %collective-permute-start = (f32[2,16,4,256]{3,2,1,0:T(4,128)S(1)}, f32[2,16,4,256]{3,2,1,0:T(4,128)S(1)}, u32[]{:S(2)}, u32[]{:S(2)}) collective-permute-start(f32[2,16,4,256]{3,2,1,0:T(4,128)S(1)} %shard_map.49.first_ref), channel_id=1, source_target_pairs={{0,63},{1,0},{2,1},{3,2},{4,3},{5,4},{6,5},{7,6},{8,7},{9,8},{10,9... | collective-permute-start | bytes 393224 | tf_op jit(solution)/shard_map/ppermute | solution.py:250
  11.2 6.1 %collective-permute-start.2 = (f32[16,128]{1,0:T(8,128)S(1)}, f32[16,128]{1,0:T(8,128)S(1)}, u32[]{:S(2)}, u32[]{:S(2)}) collective-permute-start(f32[16,128]{1,0:T(8,128)S(1)} %shard_map.51.edge_ref), channel_id=1, source_target_pairs={{64,128},{192,256},{320,384},{448,512},{576,640},{704,768},{832,89... | collective-permute-start | bytes 24584 | tf_op jit(solution)/shard_map/ppermute | solution.py:256
  13.1 4.5 %collective-permute-start.1 = (f32[16,128]{1,0:T(8,128)S(1)}, f32[16,128]{1,0:T(8,128)S(1)}, u32[]{:S(2)}, u32[]{:S(2)}) collective-permute-start(f32[16,128]{1,0:T(8,128)S(1)} %shard_map.51.edge_ref), channel_id=1, source_target_pairs={{0,64},{128,192},{256,320},{384,448},{512,576},{640,704},{768,832}... | collective-permute-start | bytes 24584 | tf_op jit(solution)/shard_map/ppermute | solution.py:257
  18.9 46.7 %all-to-all-start = ((f32[64,2,128]{2,1,0:T(2,128)}), f32[64,2,128]{2,1,0:T(2,128)S(1)}, u32[]{:S(2)}, u32[]{:S(2)}) async-start(f32[64,2,128]{2,1,0:T(2,128)} %bitcast), calls=%async_computation | async-start | bytes 131072 | tf_op jit(solution)/shard_map/all_to_all | solution.py:267
  49.8 7.7 %collective-permute-start.3 = (f32[2,16,2,256]{3,2,1,0:T(2,128)S(1)}, f32[2,16,2,256]{3,2,1,0:T(2,128)S(1)}, u32[]{:S(2)}, u32[]{:S(2)}) collective-permute-start(f32[2,16,2,256]{3,2,1,0:T(2,128)S(1)} %get-tuple-element.15), channel_id=1, source_target_pairs={{0,1},{1,2},{2,3},{3,4},{4,5},{5,6},{6,7},{7,8},{8,9},{9,10},{10,1... | collective-permute-start | bytes 196616 | tf_op jit(solution)/shard_map/ppermute | solution.py:264

commit v8 on v7

--- a/solution.py
+++ b/solution.py
@@ -25,7 +25,7 @@
     return lax.axis_index(axis) % 2 == 1
 
 
-def slice_kernel(u_hbm, v_hbm, first_ref, u_ref, v_ref, sems):
+def slice_kernel(u_hbm, v_hbm, first_ref, ready_ref, u_ref, v_ref, sems):
     part, some = planes // 2, pl.ds(0, 4)
     copies = []
     for f, (src, dst) in enumerate(((u_hbm, u_ref), (v_hbm, v_ref))):
@@ -38,10 +38,11 @@
         copy.wait()
         at = slice(h * part, h * part + part)
         first_ref[f, at] = (u_ref, v_ref)[f][at, 0:4, :]
-
-
-def fetch_kernel(u_hbm, v_hbm, first_ref, u_ref, v_ref, sems):
-    del first_ref
+    ready_ref[...] = first_ref[0, 0, 0:1, 0:128]
+
+
+def fetch_kernel(u_hbm, v_hbm, ready_ref, u_ref, v_ref, sems):
+    del ready_ref
     copies = [
         pltpu.make_async_copy(src, dst, sems.at[f])
         for f, (src, dst) in enumerate(((u_hbm, u_ref), (v_hbm, v_ref)))
@@ -243,15 +244,15 @@
 def body(u, v):
     brick = shape(planes, cols, rows)
     inside = pltpu.VMEM((planes, cols, rows), f32)
-    first = call(
-        slice_kernel, pltpu.VMEM((2, planes, 4, rows), f32), [(planes, cols, rows)] * 2, [(2, 2)],
+    first, ready = call(
+        slice_kernel, (pltpu.VMEM((2, planes, 4, rows), f32), shape(1, 128)), [(planes, cols, rows)] * 2, [(2, 2)],
         limit=large, in_specs=[pl.BlockSpec(memory_space=pltpu.HBM)] * 2,
     )(u, v)
     after = lax.ppermute(first, "gy", ring("gy", -1))
     u, v = call(
         fetch_kernel, (inside, inside), sems=[(2,)], limit=large,
         in_specs=[pl.BlockSpec(memory_space=pltpu.HBM)] * 2 + [pl.BlockSpec(memory_space=pl.ANY)],
-    )(u, v, first)
+    )(u, v, ready)
     edge = call(edge_kernel, shape(16, 128), [(2 * planes, 2, 16, 128)])(u, v, after)
     far = lax.ppermute(edge, "gx", pairs("gx", 1))
     near = lax.ppermute(edge, "gx", pairs("gx", 0))

time: 67.5 us -> 68 us (level)
  no operation moved by 1% of the time
where the time goes in v8:
time: 68 us; the launch traced here: 67.2 us
  starting transfers between devices  45.4 us (67%)
  waiting for transfers between devices  15 us (22%)
  Pallas kernels  6.11 us (9%)
  between operations  0.7 us (1%)
    all_to_all x1, starting transfers between devices, body(): lax.all_to_all(send.reshape(owners, 2, 128), 'gy', 0, 0, tiled=True, axis...  30.9 us
    all_to_all x1, waiting for transfers between devices, body(): lax.all_to_all(send.reshape(owners, 2, 128), 'gy', 0, 0, tiled=True, axis...  7.32 us
    ppermute x1, starting transfers between devices, body(): back = lax.ppermute(back, 'gy', ring('gy', 1))  5.78 us
    ppermute x1, waiting for transfers between devices, body(): after = lax.ppermute(first, 'gy', ring('gy', -1))  5.39 us
    ppermute x1, starting transfers between devices, body(): near = lax.ppermute(edge, 'gx', pairs('gx', 0))  3.68 us
    ppermute x1, starting transfers between devices, body(): after = lax.ppermute(first, 'gy', ring('gy', -1))  3.14 us
    ppermute x1, starting transfers between devices, body(): far = lax.ppermute(edge, 'gx', pairs('gx', 1))  1.91 us
    ppermute x1, waiting for transfers between devices, body(): back = lax.ppermute(back, 'gy', ring('gy', 1))  1.9 us
  transfers between devices with their start and end apart: 5, of which 4 were waited for; matrix products, arithmetic and copies ran while one was open for 0% of the time, Pallas kernels for 3%

profile of v8, /device:TPU:24, one launch (start us, length us, event | category | flops | bytes accessed | tf_op | source)
XLA Modules:
  0.0 67.2 jit_solution(6177762546342798748)
XLA Ops:
  0.6 1.4 %shard_map.49 = (f32[2,16,4,256]{3,2,1,0:T(4,128)S(1)}, f32[1,128]{1,0:T(1,128)}) custom-call(f32[16,8,256]{2,1,0:T(8,128)} %u_hbm.3, f32[16,8,256]{2,1,0:T(8,128)} %v_hbm.3), custom_call_target="tpu_custom_call" | custom-call | tf_op jit(solution)/shard_map/pallas_call | solution.py:247
  2.0 3.1 %collective-permute-start = (f32[2,16,4,256]{3,2,1,0:T(4,128)S(1)}, f32[2,16,4,256]{3,2,1,0:T(4,128)S(1)}, u32[]{:S(2)}, u32[]{:S(2)}) collective-permute-start(f32[2,16,4,256]{3,2,1,0:T(4,128)S(1)} %get-tuple-element.16), channel_id=1, source_target_pairs={{0,63},{1,0},{2,1},{3,2},{4,3},{5,4},{6,5},{7,6},{8,7},{9,8},{10,9... | collective-permute-start | bytes 393224 | tf_op jit(solution)/shard_map/ppermute | solution.py:251
  5.1 1.0 %shard_map.50 = (f32[16,8,256]{2,1,0:T(8,128)S(1)}, f32[16,8,256]{2,1,0:T(8,128)S(1)}) custom-call(f32[16,8,256]{2,1,0:T(8,128)} %u_hbm.3, f32[16,8,256]{2,1,0:T(8,128)} %v_hbm.3, f32[1,128]{1,0:T(1,128)} %get-tuple-element.13.ready_ref), custom_call_target="tpu_custom_call" | custom-call | tf_op jit(solution)/shard_map/pallas_call | solution.py:252
  6.1 5.4 %collective-permute-done.next_ref = f32[2,16,4,256]{3,2,1,0:T(4,128)S(1)} collective-permute-done((f32[2,16,4,256]{3,2,1,0:T(4,128)S(1)}, f32[2,16,4,256]{3,2,1,0:T(4,128)S(1)}, u32[]{:S(2)}, u32[]{:S(2)}) %collective-permute-start) | collective-permute-done | bytes 131104 | tf_op jit(solution)/shard_map/ppermute | solution.py:251
  11.5 0.2 shard_map.51.edge_ref
  11.7 1.9 %collective-permute-start.2 = (f32[16,128]{1,0:T(8,128)S(1)}, f32[16,128]{1,0:T(8,128)S(1)}, u32[]{:S(2)}, u32[]{:S(2)}) collective-permute-start(f32[16,128]{1,0:T(8,128)S(1)} %shard_map.51.edge_ref), channel_id=1, source_target_pairs={{64,128},{192,256},{320,384},{448,512},{576,640},{704,768},{832,89... | collective-permute-start | bytes 24584 | tf_op jit(solution)/shard_map/ppermute | solution.py:257
  13.6 3.7 %collective-permute-start.1 = (f32[16,128]{1,0:T(8,128)S(1)}, f32[16,128]{1,0:T(8,128)S(1)}, u32[]{:S(2)}, u32[]{:S(2)}) collective-permute-start(f32[16,128]{1,0:T(8,128)S(1)} %shard_map.51.edge_ref), channel_id=1, source_target_pairs={{0,64},{128,192},{256,320},{384,448},{512,576},{640,704},{768,832}... | collective-permute-start | bytes 24584 | tf_op jit(solution)/shard_map/ppermute | solution.py:258
  17.3 0.4 shard_map.52.mid_ref
  17.8 0.0 collective-permute-done.2.far_ref
  17.8 0.3 collective-permute-done.1.near_ref
  18.1 1.3 %shard_map.53 = (f32[16,8,256]{2,1,0:T(8,128)S(1)}, f32[16,8,256]{2,1,0:T(8,128)S(1)}, f32[2,16,2,256]{3,2,1,0:T(2,128)S(1)}, f32[128,128]{1,0:T(8,128)}) custom-call(f32[2,16,16,256]{3,2,1,0:T(8,128)S(1)} %shard_map.52.mid_ref, f32[16,128]{1,0:T(8,128)S(1)} %shard_map.51.edge_ref, f32[16,128]{1,0:T(8,128)S(1)} %collective-permute-done.1.near_ref, ...), custom_call_target="tpu_custom_call" | custom-call | tf_op jit(solution)/shard_map/pallas_call | solution.py:261
  19.4 30.9 %all-to-all-start = ((f32[64,2,128]{2,1,0:T(2,128)}), f32[64,2,128]{2,1,0:T(2,128)S(1)}, u32[]{:S(2)}, u32[]{:S(2)}) async-start(f32[64,2,128]{2,1,0:T(2,128)} %bitcast), calls=%async_computation | async-start | bytes 131072 | tf_op jit(solution)/shard_map/all_to_all | solution.py:268
  50.3 5.8 %collective-permute-start.3 = (f32[2,16,2,256]{3,2,1,0:T(2,128)S(1)}, f32[2,16,2,256]{3,2,1,0:T(2,128)S(1)}, u32[]{:S(2)}, u32[]{:S(2)}) collective-permute-start(f32[2,16,2,256]{3,2,1,0:T(2,128)S(1)} %get-tuple-element.19), channel_id=1, source_target_pairs={{0,1},{1,2},{2,3},{3,4},{4,5},{5,6},{6,7},{7,8},{8,9},{9,10},{10,1... | collective-permute-start | bytes 196616 | tf_op jit(solution)/shard_map/ppermute | solution.py:265
  56.1 1.9 %collective-permute-done.3.back_ref = f32[2,16,2,256]{3,2,1,0:T(2,128)S(1)} collective-permute-done((f32[2,16,2,256]{3,2,1,0:T(2,128)S(1)}, f32[2,16,2,256]{3,2,1,0:T(2,128)S(1)}, u32[]{:S(2)}, u32[]{:S(2)}) %collective-permute-start.3) | collective-permute-done | bytes 65568 | tf_op jit(solution)/shard_map/ppermute | solution.py:265
  58.0 0.8 %shard_map.54 = (f32[16,8,256]{2,1,0:T(8,128)}, f32[16,8,256]{2,1,0:T(8,128)}) custom-call(f32[16,8,256]{2,1,0:T(8,128)S(1)} %get-tuple-element.17.un_ref, f32[16,8,256]{2,1,0:T(8,128)S(1)} %get-tuple-element.18.vn_ref, f32[2,16,2,256]{3,2,1,0:T(2,128)S(1)} %collective-permute-done.3.back_ref), custom_call_target="tpu_custom_call" | custom-call | tf_op jit(solution)/shard_map/pallas_call | solution.py:266
  58.7 7.3 %all-to-all-done = f32[64,2,128]{2,1,0:T(2,128)S(1)} async-done(((f32[64,2,128]{2,1,0:T(2,128)}), f32[64,2,128]{2,1,0:T(2,128)S(1)}, u32[]{:S(2)}, u32[]{:S(2)}) %all-to-all-start) | async-done | bytes 65568 | tf_op jit(solution)/shard_map/all_to_all | solution.py:268
  66.1 1.1 %shard_map.55 = f32[32,16,128]{2,1,0:T(8,128)} custom-call(f32[128,128]{1,0:T(8,128)S(1)} %bitcast.7), custom_call_target="tpu_custom_call" | custom-call | tf_op jit(solution)/shard_map/pallas_call | solution.py:271
Async XLA Ops:
  2.0 9.5 %collective-permute-start = (f32[2,16,4,256]{3,2,1,0:T(4,128)S(1)}, f32[2,16,4,256]{3,2,1,0:T(4,128)S(1)}, u32[]{:S(2)}, u32[]{:S(2)}) collective-permute-start(f32[2,16,4,256]{3,2,1,0:T(4,128)S(1)} %get-tuple-element.16), channel_id=1, source_target_pairs={{0,63},{1,0},{2,1},{3,2},{4,3},{5,4},{6,5},{7,6},{8,7},{9,8},{10,9... | collective-permute-start | bytes 393224 | tf_op jit(solution)/shard_map/ppermute | solution.py:251
  11.7 6.1 %collective-permute-start.2 = (f32[16,128]{1,0:T(8,128)S(1)}, f32[16,128]{1,0:T(8,128)S(1)}, u32[]{:S(2)}, u32[]{:S(2)}) collective-permute-start(f32[16,128]{1,0:T(8,128)S(1)} %shard_map.51.edge_ref), channel_id=1, source_target_pairs={{64,128},{192,256},{320,384},{448,512},{576,640},{704,768},{832,89... | collective-permute-start | bytes 24584 | tf_op jit(solution)/shard_map/ppermute | solution.py:257
  13.6 4.5 %collective-permute-start.1 = (f32[16,128]{1,0:T(8,128)S(1)}, f32[16,128]{1,0:T(8,128)S(1)}, u32[]{:S(2)}, u32[]{:S(2)}) collective-permute-start(f32[16,128]{1,0:T(8,128)S(1)} %shard_map.51.edge_ref), channel_id=1, source_target_pairs={{0,64},{128,192},{256,320},{384,448},{512,576},{640,704},{768,832}... | collective-permute-start | bytes 24584 | tf_op jit(solution)/shard_map/ppermute | solution.py:258
  19.4 46.7 %all-to-all-start = ((f32[64,2,128]{2,1,0:T(2,128)}), f32[64,2,128]{2,1,0:T(2,128)S(1)}, u32[]{:S(2)}, u32[]{:S(2)}) async-start(f32[64,2,128]{2,1,0:T(2,128)} %bitcast), calls=%async_computation | async-start | bytes 131072 | tf_op jit(solution)/shard_map/all_to_all | solution.py:268
  50.3 7.7 %collective-permute-start.3 = (f32[2,16,2,256]{3,2,1,0:T(2,128)S(1)}, f32[2,16,2,256]{3,2,1,0:T(2,128)S(1)}, u32[]{:S(2)}, u32[]{:S(2)}) collective-permute-start(f32[2,16,2,256]{3,2,1,0:T(2,128)S(1)} %get-tuple-element.19), channel_id=1, source_target_pairs={{0,1},{1,2},{2,3},{3,4},{4,5},{5,6},{6,7},{7,8},{8,9},{9,10},{10,1... | collective-permute-start | bytes 196616 | tf_op jit(solution)/shard_map/ppermute | solution.py:265

commit v9 on v7

--- a/solution.py
+++ b/solution.py
@@ -13,7 +13,7 @@
 planes, cols, rows = 16, 8, 256
 owners = 64
 large = 56 * 1024 * 1024
-master = 45
+master = 47
 f32 = jnp.float32
 
 

time: 67.5 us -> 67.3 us (level)
  starting transfers between devices: 45.4 us -> 44.7 us
    all_to_all x1, starting transfers between devices: 30.9 us -> 30.2 us  [body(): lax.all_to_all(send.reshape(owners, 2, 128), 'gy', 0, 0, tiled=True, axis...]
where the time goes in v9:
time: 67.3 us; the launch traced here: 66.5 us
  starting transfers between devices  44.7 us (66%)
  waiting for transfers between devices  15.5 us (23%)
  Pallas kernels  5.6 us (8%)
  between operations  0.72 us (1%)
    all_to_all x1, starting transfers between devices, body(): lax.all_to_all(send.reshape(owners, 2, 128), 'gy', 0, 0, tiled=True, axis...  30.2 us
    all_to_all x1, waiting for transfers between devices, body(): lax.all_to_all(send.reshape(owners, 2, 128), 'gy', 0, 0, tiled=True, axis...  7.84 us
    ppermute x1, starting transfers between devices, body(): back = lax.ppermute(back, 'gy', ring('gy', 1))  5.78 us
    ppermute x1, waiting for transfers between devices, body(): after = lax.ppermute(first, 'gy', ring('gy', -1))  5.38 us
    ppermute x1, starting transfers between devices, body(): near = lax.ppermute(edge, 'gx', pairs('gx', 0))  3.68 us
    ppermute x1, starting transfers between devices, body(): after = lax.ppermute(first, 'gy', ring('gy', -1))  3.14 us
    ppermute x1, waiting for transfers between devices, body(): back = lax.ppermute(back, 'gy', ring('gy', 1))  1.91 us
    ppermute x1, starting transfers between devices, body(): far = lax.ppermute(edge, 'gx', pairs('gx', 1))  1.91 us
  transfers between devices with their start and end apart: 5, of which 4 were waited for; matrix products, arithmetic and copies ran while one was open for 0% of the time, Pallas kernels for 3%

profile of v9, /device:TPU:24, one launch (start us, length us, event | category | flops | bytes accessed | tf_op | source)
XLA Modules:
  0.0 66.5 jit_solution(9589951930396312683)
XLA Ops:
  0.6 0.8 %shard_map.49.first_ref = f32[2,16,4,256]{3,2,1,0:T(4,128)S(1)} custom-call(f32[16,8,256]{2,1,0:T(8,128)} %u_hbm.3, f32[16,8,256]{2,1,0:T(8,128)} %v_hbm.3), custom_call_target="tpu_custom_call" | custom-call | tf_op jit(solution)/shard_map/pallas_call | solution.py:246
  1.5 0.0 copy-start
  1.5 3.1 %collective-permute-start = (f32[2,16,4,256]{3,2,1,0:T(4,128)S(1)}, f32[2,16,4,256]{3,2,1,0:T(4,128)S(1)}, u32[]{:S(2)}, u32[]{:S(2)}) collective-permute-start(f32[2,16,4,256]{3,2,1,0:T(4,128)S(1)} %shard_map.49.first_ref), channel_id=1, source_target_pairs={{0,63},{1,0},{2,1},{3,2},{4,3},{5,4},{6,5},{7,6},{8,7},{9,8},{10,9... | collective-permute-start | bytes 393224 | tf_op jit(solution)/shard_map/ppermute | solution.py:250
  4.6 0.0 copy-done
  4.7 1.0 %shard_map.50 = (f32[16,8,256]{2,1,0:T(8,128)S(1)}, f32[16,8,256]{2,1,0:T(8,128)S(1)}) custom-call(f32[16,8,256]{2,1,0:T(8,128)} %u_hbm.3, f32[16,8,256]{2,1,0:T(8,128)} %v_hbm.3, f32[2,16,4,256]{3,2,1,0:T(4,128)} %copy-done), custom_call_target="tpu_custom_call" | custom-call | tf_op jit(solution)/shard_map/pallas_call | solution.py:251
  5.7 5.4 %collective-permute-done.next_ref = f32[2,16,4,256]{3,2,1,0:T(4,128)S(1)} collective-permute-done((f32[2,16,4,256]{3,2,1,0:T(4,128)S(1)}, f32[2,16,4,256]{3,2,1,0:T(4,128)S(1)}, u32[]{:S(2)}, u32[]{:S(2)}) %collective-permute-start) | collective-permute-done | bytes 131104 | tf_op jit(solution)/shard_map/ppermute | solution.py:250
  11.0 0.2 shard_map.51.edge_ref
  11.2 1.9 %collective-permute-start.2 = (f32[16,128]{1,0:T(8,128)S(1)}, f32[16,128]{1,0:T(8,128)S(1)}, u32[]{:S(2)}, u32[]{:S(2)}) collective-permute-start(f32[16,128]{1,0:T(8,128)S(1)} %shard_map.51.edge_ref), channel_id=1, source_target_pairs={{64,128},{192,256},{320,384},{448,512},{576,640},{704,768},{832,89... | collective-permute-start | bytes 24584 | tf_op jit(solution)/shard_map/ppermute | solution.py:256
  13.1 3.7 %collective-permute-start.1 = (f32[16,128]{1,0:T(8,128)S(1)}, f32[16,128]{1,0:T(8,128)S(1)}, u32[]{:S(2)}, u32[]{:S(2)}) collective-permute-start(f32[16,128]{1,0:T(8,128)S(1)} %shard_map.51.edge_ref), channel_id=1, source_target_pairs={{0,64},{128,192},{256,320},{384,448},{512,576},{640,704},{768,832}... | collective-permute-start | bytes 24584 | tf_op jit(solution)/shard_map/ppermute | solution.py:257
  16.8 0.4 shard_map.52.mid_ref
  17.3 0.0 collective-permute-done.2.far_ref
  17.3 0.3 collective-permute-done.1.near_ref
  17.6 1.3 %shard_map.53 = (f32[16,8,256]{2,1,0:T(8,128)S(1)}, f32[16,8,256]{2,1,0:T(8,128)S(1)}, f32[2,16,2,256]{3,2,1,0:T(2,128)S(1)}, f32[128,128]{1,0:T(8,128)}) custom-call(f32[2,16,16,256]{3,2,1,0:T(8,128)S(1)} %shard_map.52.mid_ref, f32[16,128]{1,0:T(8,128)S(1)} %shard_map.51.edge_ref, f32[16,128]{1,0:T(8,128)S(1)} %collective-permute-done.1.near_ref, ...), custom_call_target="tpu_custom_call" | custom-call | tf_op jit(solution)/shard_map/pallas_call | solution.py:260
  18.9 30.2 %all-to-all-start = ((f32[64,2,128]{2,1,0:T(2,128)}), f32[64,2,128]{2,1,0:T(2,128)S(1)}, u32[]{:S(2)}, u32[]{:S(2)}) async-start(f32[64,2,128]{2,1,0:T(2,128)} %bitcast), calls=%async_computation | async-start | bytes 131072 | tf_op jit(solution)/shard_map/all_to_all | solution.py:267
  49.1 5.8 %collective-permute-start.3 = (f32[2,16,2,256]{3,2,1,0:T(2,128)S(1)}, f32[2,16,2,256]{3,2,1,0:T(2,128)S(1)}, u32[]{:S(2)}, u32[]{:S(2)}) collective-permute-start(f32[2,16,2,256]{3,2,1,0:T(2,128)S(1)} %get-tuple-element.15), channel_id=1, source_target_pairs={{0,1},{1,2},{2,3},{3,4},{4,5},{5,6},{6,7},{7,8},{8,9},{9,10},{10,1... | collective-permute-start | bytes 196616 | tf_op jit(solution)/shard_map/ppermute | solution.py:264
  54.9 1.9 %collective-permute-done.3.back_ref = f32[2,16,2,256]{3,2,1,0:T(2,128)S(1)} collective-permute-done((f32[2,16,2,256]{3,2,1,0:T(2,128)S(1)}, f32[2,16,2,256]{3,2,1,0:T(2,128)S(1)}, u32[]{:S(2)}, u32[]{:S(2)}) %collective-permute-start.3) | collective-permute-done | bytes 65568 | tf_op jit(solution)/shard_map/ppermute | solution.py:264
  56.8 0.8 %shard_map.54 = (f32[16,8,256]{2,1,0:T(8,128)}, f32[16,8,256]{2,1,0:T(8,128)}) custom-call(f32[16,8,256]{2,1,0:T(8,128)S(1)} %get-tuple-element.13.un_ref, f32[16,8,256]{2,1,0:T(8,128)S(1)} %get-tuple-element.14.vn_ref, f32[2,16,2,256]{3,2,1,0:T(2,128)S(1)} %collective-permute-done.3.back_ref), custom_call_target="tpu_custom_call" | custom-call | tf_op jit(solution)/shard_map/pallas_call | solution.py:265
  57.6 7.8 %all-to-all-done = f32[64,2,128]{2,1,0:T(2,128)S(1)} async-done(((f32[64,2,128]{2,1,0:T(2,128)}), f32[64,2,128]{2,1,0:T(2,128)S(1)}, u32[]{:S(2)}, u32[]{:S(2)}) %all-to-all-start) | async-done | bytes 65568 | tf_op jit(solution)/shard_map/all_to_all | solution.py:267
  65.4 1.1 %shard_map.55 = f32[32,16,128]{2,1,0:T(8,128)} custom-call(f32[128,128]{1,0:T(8,128)S(1)} %bitcast.7), custom_call_target="tpu_custom_call" | custom-call | tf_op jit(solution)/shard_map/pallas_call | solution.py:270
Async XLA Ops:
  1.5 3.2 %copy-start = (f32[2,16,4,256]{3,2,1,0:T(4,128)}, f32[2,16,4,256]{3,2,1,0:T(4,128)S(1)}, u32[]{:S(2)}) copy-start(f32[2,16,4,256]{3,2,1,0:T(4,128)S(1)} %shard_map.49.first_ref) | copy-start | bytes 393220
  1.5 9.5 %collective-permute-start = (f32[2,16,4,256]{3,2,1,0:T(4,128)S(1)}, f32[2,16,4,256]{3,2,1,0:T(4,128)S(1)}, u32[]{:S(2)}, u32[]{:S(2)}) collective-permute-start(f32[2,16,4,256]{3,2,1,0:T(4,128)S(1)} %shard_map.49.first_ref), channel_id=1, source_target_pairs={{0,63},{1,0},{2,1},{3,2},{4,3},{5,4},{6,5},{7,6},{8,7},{9,8},{10,9... | collective-permute-start | bytes 393224 | tf_op jit(solution)/shard_map/ppermute | solution.py:250
  11.2 6.1 %collective-permute-start.2 = (f32[16,128]{1,0:T(8,128)S(1)}, f32[16,128]{1,0:T(8,128)S(1)}, u32[]{:S(2)}, u32[]{:S(2)}) collective-permute-start(f32[16,128]{1,0:T(8,128)S(1)} %shard_map.51.edge_ref), channel_id=1, source_target_pairs={{64,128},{192,256},{320,384},{448,512},{576,640},{704,768},{832,89... | collective-permute-start | bytes 24584 | tf_op jit(solution)/shard_map/ppermute | solution.py:256
  13.1 4.5 %collective-permute-start.1 = (f32[16,128]{1,0:T(8,128)S(1)}, f32[16,128]{1,0:T(8,128)S(1)}, u32[]{:S(2)}, u32[]{:S(2)}) collective-permute-start(f32[16,128]{1,0:T(8,128)S(1)} %shard_map.51.edge_ref), channel_id=1, source_target_pairs={{0,64},{128,192},{256,320},{384,448},{512,576},{640,704},{768,832}... | collective-permute-start | bytes 24584 | tf_op jit(solution)/shard_map/ppermute | solution.py:257
  18.9 46.5 %all-to-all-start = ((f32[64,2,128]{2,1,0:T(2,128)}), f32[64,2,128]{2,1,0:T(2,128)S(1)}, u32[]{:S(2)}, u32[]{:S(2)}) async-start(f32[64,2,128]{2,1,0:T(2,128)} %bitcast), calls=%async_computation | async-start | bytes 131072 | tf_op jit(solution)/shard_map/all_to_all | solution.py:267
  49.1 7.7 %collective-permute-start.3 = (f32[2,16,2,256]{3,2,1,0:T(2,128)S(1)}, f32[2,16,2,256]{3,2,1,0:T(2,128)S(1)}, u32[]{:S(2)}, u32[]{:S(2)}) collective-permute-start(f32[2,16,2,256]{3,2,1,0:T(2,128)S(1)} %get-tuple-element.15), channel_id=1, source_target_pairs={{0,1},{1,2},{2,3},{3,4},{4,5},{5,6},{6,7},{7,8},{8,9},{9,10},{10,1... | collective-permute-start | bytes 196616 | tf_op jit(solution)/shard_map/ppermute | solution.py:264
